TPU v7x, 512 devices: a whole 4x8x8 slice. The times are simulated.
512 devices in a mesh: seq: 64 (over x, z, core), fsdp: 8 (over y).
Axes of the slice: x: 4, y: 8, z: 8, core: 2. Of those that a mesh axis runs over, the one named last changes fastest.
Arguments:
- query: bfloat16 [8, 8192, 2048], P('fsdp', 'seq'), may hold values from -100 to 100
- key_proj: bfloat16 [8, 8192, 512], P('fsdp', 'seq'), may hold values from -4 to 4
- value_projection_side: bfloat16 [8, 8192, 512], P('fsdp', 'seq'), may hold values from -6 to 6
- residual: bfloat16 [8, 8192, 2048], P('fsdp', 'seq'), may hold values from -6 to 6
- w_out: bfloat16 [2048, 2048], P('fsdp'), may hold values from -0.125 to 0.125
- doc_ids: int32 [8, 8192], P('fsdp'), may hold values from 0 to 31, as said below
- slot_token: int32 [8, 163840], P('fsdp', 'seq'), may hold values from -1 to 8191, as said below
- head_of: int32 [64], replicated, may hold values from 0 to 15, as said below
Outputs:
- layer_out: bfloat16 [8, 8192, 2048], P('fsdp', 'seq')
- slot_stats: float32 [8, 163840], P('fsdp', 'seq')
Inputs may be any that keep to these rules, and one draw needn't show every extreme that they name: `doc_ids`: never falling along the pack; each document holds between one half and one and a half times 256 tokens. `slot_token`: the indices of seq form groups of 16 in a row. Each document of a pack belongs to one group, and every device of that group holds all tokens of all documents of its group in its first slots, in increasing order, and -1 in the rest. `head_of`: within each group of 16 indices of seq in a row, every head once.
All inputs are finite; a program needn't handle non-finite values.
Results may differ from a plain program's by a relative error of at most 0.0034.
Values may be sent and summed in bfloat16 or wider, within the bound.
No kernel may reach another device: no remote copies, remote signals or barrier semaphores. Data moves between devices by JAX's collectives and lax.ppermute only.
A program may use at most 64 MiB of HBM per device.

v0:
```python
import math

import jax
import jax.numpy as jnp
from jax import lax
from jax.sharding import PartitionSpec as P

HEAD_SIZE = 128


def local(query, key_proj, value_projection_side, residual, w_out, doc_ids, slot_token, head_of):
    seq_count = lax.axis_size("seq")
    tok_rows = query.shape[1]
    row_count_total = tok_rows * seq_count
    heads = query.shape[2] // HEAD_SIZE
    kv_heads = key_proj.shape[2] // HEAD_SIZE
    query_per_key_group = heads // kv_heads
    score_scale = 1.0 / math.sqrt(HEAD_SIZE)
    query_heads = query[0].reshape(tok_rows, heads, HEAD_SIZE)
    key_head_split = key_proj[0].reshape(tok_rows, kv_heads, HEAD_SIZE)
    value_head_split = value_projection_side[0].reshape(tok_rows, kv_heads, HEAD_SIZE)
    kv_choice = head_of // query_per_key_group
    payload = jnp.concatenate(
        [
            jnp.take(query_heads, head_of, axis=1),
            jnp.take(key_head_split, kv_choice, axis=1),
            jnp.take(value_head_split, kv_choice, axis=1),
        ],
        axis=2,
    )
    slots = slot_token[0]
    capacity = slots.shape[0]
    live = slots >= 0
    safe_tokens = jnp.maximum(slots, 0)
    arrived = lax.all_to_all(payload, "seq", split_axis=1, concat_axis=0, tiled=True).reshape(
        row_count_total, 3 * HEAD_SIZE
    )
    picked = jnp.take(arrived, safe_tokens, axis=0)
    slot_docs = jnp.where(live, jnp.take(doc_ids[0], safe_tokens), -1)
    query_slots = picked[:, :HEAD_SIZE]
    key_slots = picked[:, HEAD_SIZE : 2 * HEAD_SIZE]
    value_slots = picked[:, 2 * HEAD_SIZE :]
    block = math.gcd(capacity, 512)

    def one_block(begin_row):
        key_start = jnp.clip(begin_row + block - capacity, 0, capacity - capacity)
        query_block = lax.dynamic_slice_in_dim(query_slots, begin_row, block, 0)
        query_docs = lax.dynamic_slice_in_dim(slot_docs, begin_row, block, 0)
        query_pos = begin_row + jnp.arange(block, dtype=jnp.int32)
        key_pos = key_start + jnp.arange(capacity, dtype=jnp.int32)
        scores = (
            lax.dot_general(
                query_block, key_slots, (((1,), (1,)), ((), ())), preferred_element_type=jnp.float32
            )
            * score_scale
        )
        allowed = (
            (query_docs[:, None] == slot_docs[None, :])
            & (slot_docs[None, :] >= 0)
            & (key_pos[None, :] <= query_pos[:, None])
        )
        scores = jnp.where(allowed, scores, -jnp.inf)
        has_keys = jnp.any(allowed, axis=1)
        top = jnp.where(has_keys, jnp.max(scores, axis=1), 0.0)
        weights = jnp.where(allowed, jnp.exp(scores - top[:, None]), 0.0)
        totals = jnp.where(has_keys, jnp.sum(weights, axis=1), 1.0)
        share = (weights / totals[:, None]).astype(jnp.bfloat16)
        mixed = jnp.dot(share, value_slots, preferred_element_type=jnp.float32).astype(jnp.bfloat16)
        log_total = jnp.where(has_keys, top + jnp.log(totals), 0.0)
        return (mixed, log_total)

    starts = jnp.arange(capacity // block, dtype=jnp.int32) * block
    mixed_blocks, stat_blocks = lax.map(one_block, starts)
    mixed_slots = mixed_blocks.reshape(capacity, HEAD_SIZE)
    slot_stats = stat_blocks.reshape(1, capacity)
    back_rows = (
        jnp.zeros((row_count_total, HEAD_SIZE), jnp.bfloat16)
        .at[jnp.where(live, slots, row_count_total)]
        .set(mixed_slots, mode="drop")
    )
    returned = lax.all_to_all(
        back_rows.reshape(row_count_total, 1, HEAD_SIZE),
        "seq",
        split_axis=0,
        concat_axis=1,
        tiled=True,
    )
    chooser = (head_of[:, None] == jnp.arange(heads, dtype=jnp.int32)[None, :]).astype(jnp.bfloat16)
    attended = jnp.einsum("rsd,sh->rhd", returned, chooser, preferred_element_type=jnp.float32)
    attended = attended.astype(jnp.bfloat16).reshape(tok_rows, heads * HEAD_SIZE)
    projected = jnp.dot(
        attended,
        lax.all_gather(w_out, "fsdp", axis=0, tiled=True),
        preferred_element_type=jnp.float32,
    )
    layer_out = (residual[0].astype(jnp.float32) + projected).astype(jnp.bfloat16)[None]
    return (layer_out, slot_stats)


def solution(mesh):
    return jax.shard_map(
        local,
        mesh=mesh,
        in_specs=(
            P("fsdp", "seq", None),
            P("fsdp", "seq", None),
            P("fsdp", "seq", None),
            P("fsdp", "seq", None),
            P("fsdp", None),
            P("fsdp", None),
            P("fsdp", "seq"),
            P(),
        ),
        out_specs=(P("fsdp", "seq", None), P("fsdp", "seq")),
        check_vma=False,
    )
```

profile of v0, /device:TPU:1, one launch (start us, length us, event | category | flops | bytes accessed | tf_op | source)
XLA Modules:
  0.0 362.1 jit_solution(6601956589336359544)
XLA Ops:
  7.2 0.7 compare_and_fusion.2
  7.9 0.7 compare_select_fusion.6
  8.5 1.0 copy.27
  9.5 0.1 copy.28
  9.7 1.0 copy.29
  10.7 0.1 copy.30
  10.9 1.0 gather_fusion.3
  11.8 2.2 gather_fusion.4
  14.0 1.3 copy.25
  15.3 0.3 copy.26
  15.6 2.1 gather_fusion.1
  17.7 2.6 select_bitcast_fusion.1
  20.3 3.4 pad_maximum_fusion
  23.7 15.1 %all-to-all-start = ((bf16[128,64,384]{2,0,1:T(8,128)(2,1)}), bf16[128,64,384]{2,0,1:T(8,128)(2,1)}, u32[]{:S(2)}, u32[]{:S(2)}) async-start(bf16[128,64,384]{2,0,1:T(8,128)(2,1)} %pad_maximum_fusion), calls=%async_computation | async-start | bytes 12582912 | tf_op jit(solution)/shard_map/all_to_all | solution.py:35
  38.9 0.7 all-gather.2.cloned.1.call-update
  39.7 13.8 %gather_fusion = s32[2560]{0:T(1024)S(1)} fusion(s32[8192]{0:T(1024)S(1)} %bitcast.68, s32[3072]{0:T(1024)S(1)} %pad_clamp_fusion), kind=kCustom, calls=%fused_computation.2 | custom fusion | bytes 30720 | tf_op jit(solution)/shard_map/jit(_take)/gather | solution.py:39
  53.6 126.1 %all-to-all-done = bf16[128,64,384]{2,0,1:T(8,128)(2,1)} async-done(((bf16[128,64,384]{2,0,1:T(8,128)(2,1)}), bf16[128,64,384]{2,0,1:T(8,128)(2,1)}, u32[]{:S(2)}, u32[]{:S(2)}) %all-to-all-start) | async-done | bytes 6291488 | tf_op jit(solution)/shard_map/all_to_all | solution.py:35
  179.7 10.4 %gather_fusion.2 = bf16[2560,384]{1,0:T(8,128)(2,1)S(1)} fusion(bf16[8192,384]{1,0:T(8,128)(2,1)} %bitcast.16, s32[3072]{0:T(1024)S(1)} %pad_clamp_fusion), kind=kCustom, calls=%fused_computation.4 | custom fusion | bytes 3942400 | tf_op jit(solution)/shard_map/jit(_take)/gather | solution.py:38
  190.1 1.4 broadcast_select_fusion.2
  191.5 0.3 fusion.29
  191.8 74.9 %while.16 = (s32[]{:T(128)}, bf16[5,512,128]{2,1,0:T(8,128)(2,1)S(1)}, f32[5,512]{1,0:T(8,128)S(1)}, s32[5]{0:T(128)S(1)}, s32[2560]{0:T(1024)S(1)}, /*index=5*/...) while((s32[]{:T(128)}, ...), condition=%wide.region_4.6_spmd, body=%wide.region_0.5_spmd.sunk | while | flops 706550784 | bytes 38450940 | solution.py:73
  191.9 0.6 dynamic_slice.36
  195.1 0.7 iota_add_fusion.4
  195.8 2.0 fusion.41
  197.8 1.6 fusion.42
  199.4 2.5 fusion.43
  202.0 4.8 %fusion.44 = bf16[5,512,128]{2,1,0:T(8,128)(2,1)S(1)} fusion(bf16[5,512,128]{2,1,0:T(8,128)(2,1)S(1)} %get-tuple-element.263, s32[]{:T(128)} %get-tuple-element.262, bf16[2560,128]{1,0:T(8,128)(2,1)S(1)} %get-tuple-element.281, f32[512,2560]{1,0:T(8,128)} %copy-done.1, f32[512]{0:T(512)S(1)} %broadcast_select_fusion.6, ...), kind=kOutput, calls=%fused_computation.14.clone.1 | convolution fusion | flops 346095616 | bytes 6065156 | tf_op jit(solution)/shard_map/while/body/eval_jaxpr/dot_general | solution.py:68
  206.8 0.6 dynamic_slice.36
  210.1 0.7 iota_add_fusion.4
  210.8 2.0 fusion.41
  212.8 1.6 fusion.42
  214.4 2.5 fusion.43
  217.0 4.8 %fusion.44 = bf16[5,512,128]{2,1,0:T(8,128)(2,1)S(1)} fusion(bf16[5,512,128]{2,1,0:T(8,128)(2,1)S(1)} %get-tuple-element.263, s32[]{:T(128)} %get-tuple-element.262, bf16[2560,128]{1,0:T(8,128)(2,1)S(1)} %get-tuple-element.281, f32[512,2560]{1,0:T(8,128)} %copy-done.1, f32[512]{0:T(512)S(1)} %broadcast_select_fusion.6, ...), kind=kOutput, calls=%fused_computation.14.clone.1 | convolution fusion | flops 346095616 | bytes 6065156 | tf_op jit(solution)/shard_map/while/body/eval_jaxpr/dot_general | solution.py:68
  221.8 0.6 dynamic_slice.36
  224.4 0.1 dynamic_slice.37
  225.1 0.7 iota_add_fusion.4
  225.8 2.0 fusion.41
  227.8 1.6 fusion.42
  229.4 2.5 fusion.43
  232.0 4.8 %fusion.44 = bf16[5,512,128]{2,1,0:T(8,128)(2,1)S(1)} fusion(bf16[5,512,128]{2,1,0:T(8,128)(2,1)S(1)} %get-tuple-element.263, s32[]{:T(128)} %get-tuple-element.262, bf16[2560,128]{1,0:T(8,128)(2,1)S(1)} %get-tuple-element.281, f32[512,2560]{1,0:T(8,128)} %copy-done.1, f32[512]{0:T(512)S(1)} %broadcast_select_fusion.6, ...), kind=kOutput, calls=%fused_computation.14.clone.1 | convolution fusion | flops 346095616 | bytes 6065156 | tf_op jit(solution)/shard_map/while/body/eval_jaxpr/dot_general | solution.py:68
  236.8 0.6 dynamic_slice.36
  239.4 0.1 dynamic_slice.37
  240.1 0.7 iota_add_fusion.4
  240.8 2.0 fusion.41
  242.8 1.6 fusion.42
  244.4 2.5 fusion.43
  247.0 4.8 %fusion.44 = bf16[5,512,128]{2,1,0:T(8,128)(2,1)S(1)} fusion(bf16[5,512,128]{2,1,0:T(8,128)(2,1)S(1)} %get-tuple-element.263, s32[]{:T(128)} %get-tuple-element.262, bf16[2560,128]{1,0:T(8,128)(2,1)S(1)} %get-tuple-element.281, f32[512,2560]{1,0:T(8,128)} %copy-done.1, f32[512]{0:T(512)S(1)} %broadcast_select_fusion.6, ...), kind=kOutput, calls=%fused_computation.14.clone.1 | convolution fusion | flops 346095616 | bytes 6065156 | tf_op jit(solution)/shard_map/while/body/eval_jaxpr/dot_general | solution.py:68
  251.8 0.6 dynamic_slice.36
  255.1 0.7 iota_add_fusion.4
  255.8 2.0 fusion.41
  257.8 1.6 fusion.42
  259.4 2.5 fusion.43
  262.0 4.8 %fusion.44 = bf16[5,512,128]{2,1,0:T(8,128)(2,1)S(1)} fusion(bf16[5,512,128]{2,1,0:T(8,128)(2,1)S(1)} %get-tuple-element.263, s32[]{:T(128)} %get-tuple-element.262, bf16[2560,128]{1,0:T(8,128)(2,1)S(1)} %get-tuple-element.281, f32[512,2560]{1,0:T(8,128)} %copy-done.1, f32[512]{0:T(512)S(1)} %broadcast_select_fusion.6, ...), kind=kOutput, calls=%fused_computation.14.clone.1 | convolution fusion | flops 346095616 | bytes 6065156 | tf_op jit(solution)/shard_map/while/body/eval_jaxpr/dot_general | solution.py:68
  266.8 8.0 %scatter_custom_fusion = bf16[8192,128]{1,0:T(8,128)(2,1)S(1)} fusion(s32[2560]{0:T(1024)S(1)} %get-tuple-element.167, bf16[2560,128]{1,0:T(8,128)(2,1)S(1)} %bitcast.79, bf16[]{:T(256)} %constant.155.clone.1), kind=kCustom, calls=%fused_computation.41 | custom fusion | bytes 2097154 | tf_op jit(solution)/shard_map/scatter | solution.py:79
  274.8 0.5 broadcast.223
  275.3 3.0 reduce.8
  278.3 4.0 %reshape.225 = bf16[64,2,8192]{2,1,0:T(2,128)(2,1)} reshape(bf16[8192,128]{1,0:T(8,128)(2,1)} %reduce.8) | data formatting | bytes 4194304
  282.3 5.8 %all-to-all-start.1 = ((bf16[64,2,8192]{2,1,0:T(2,128)(2,1)}), bf16[64,2,8192]{2,1,0:T(2,128)(2,1)S(1)}, u32[]{:S(2)}, u32[]{:S(2)}) async-start(bf16[64,2,8192]{2,1,0:T(2,128)(2,1)} %reshape.225), calls=%async_computation.1 | async-start | bytes 4194304 | tf_op jit(solution)/shard_map/all_to_all | solution.py:81
  288.0 0.6 copy.35
  288.7 50.6 %all-to-all-done.1 = bf16[64,2,8192]{2,1,0:T(2,128)(2,1)S(1)} async-done(((bf16[64,2,8192]{2,1,0:T(2,128)(2,1)}), bf16[64,2,8192]{2,1,0:T(2,128)(2,1)S(1)}, u32[]{:S(2)}, u32[]{:S(2)}) %all-to-all-start.1) | async-done | bytes 2097184 | tf_op jit(solution)/shard_map/all_to_all | solution.py:81
  339.3 6.8 %reshape.226 = bf16[8192,1,128]{2,1,0:T(2,128)(2,1)} reshape(bf16[64,2,8192]{2,1,0:T(2,128)(2,1)S(1)} %all-to-all-done.1) | data formatting | bytes 4194304
  346.1 2.5 copy.33
  348.6 1.3 fusion.16
  349.9 5.4 %fusion.12 = bf16[1,128,2048]{2,1,0:T(8,128)(2,1)} fusion(bf16[2048,2048]{1,0:T(8,128)(2,1)} %all-gather.2.cloned.1.call-done, bf16[16,8,16,128]{3,2,1,0:T(8,128)(2,1)S(1)} %bitcast.71, bf16[1,128,2048]{2,1,0:T(8,128)(2,1)S(1)} %copy-done.2), kind=kOutput, calls=%fused_computation.32 | convolution fusion | flops 1074528256 | bytes 9961472 | tf_op jit(solution)/shard_map/dot_general | solution.py:91
  (62 shorter events, 1.0 us)
Async XLA Ops:
  7.2 32.5 %copy-start = (s32[1,8192]{1,0:T(1,128)S(1)}, s32[1,8192]{1,0:T(1,128)}, u32[]{:S(2)}) copy-start(s32[1,8192]{1,0:T(1,128)} %param.17) | copy-start | bytes 98308
  23.7 15.9 %copy-start.3 = (s32[1,2560]{1,0:T(1,128)S(1)}, s32[1,2560]{1,0:T(1,128)}, u32[]{:S(2)}) copy-start(s32[1,2560]{1,0:T(1,128)} %param.18) | copy-start | bytes 30724
  23.7 156.0 %all-to-all-start = ((bf16[128,64,384]{2,0,1:T(8,128)(2,1)}), bf16[128,64,384]{2,0,1:T(8,128)(2,1)}, u32[]{:S(2)}, u32[]{:S(2)}) async-start(bf16[128,64,384]{2,0,1:T(8,128)(2,1)} %pad_maximum_fusion), calls=%async_computation | async-start | bytes 12582912 | tf_op jit(solution)/shard_map/all_to_all | solution.py:35
  38.8 311.0 %all-gather.2.cloned.1.call-start = ((), (), s32[]{:S(2)}) async-start(), calls=%async_computation.2 | async-start | bytes 9437184 | tf_op jit(solution)/shard_map/all_gather | solution.py:93
  197.8 4.1 %copy-start.1 = (f32[512,2560]{1,0:T(8,128)}, f32[512,2560]{1,0:T(8,128)S(1)}, u32[]{:S(2)}) copy-start(f32[512,2560]{1,0:T(8,128)S(1)} %get-tuple-element.248) | copy-start | bytes 15728644 | tf_op jit(solution)/shard_map/while
  212.8 4.1 %copy-start.1 = (f32[512,2560]{1,0:T(8,128)}, f32[512,2560]{1,0:T(8,128)S(1)}, u32[]{:S(2)}) copy-start(f32[512,2560]{1,0:T(8,128)S(1)} %get-tuple-element.248) | copy-start | bytes 15728644 | tf_op jit(solution)/shard_map/while
  227.8 4.1 %copy-start.1 = (f32[512,2560]{1,0:T(8,128)}, f32[512,2560]{1,0:T(8,128)S(1)}, u32[]{:S(2)}) copy-start(f32[512,2560]{1,0:T(8,128)S(1)} %get-tuple-element.248) | copy-start | bytes 15728644 | tf_op jit(solution)/shard_map/while
  242.8 4.1 %copy-start.1 = (f32[512,2560]{1,0:T(8,128)}, f32[512,2560]{1,0:T(8,128)S(1)}, u32[]{:S(2)}) copy-start(f32[512,2560]{1,0:T(8,128)S(1)} %get-tuple-element.248) | copy-start | bytes 15728644 | tf_op jit(solution)/shard_map/while
  257.7 4.1 %copy-start.1 = (f32[512,2560]{1,0:T(8,128)}, f32[512,2560]{1,0:T(8,128)S(1)}, u32[]{:S(2)}) copy-start(f32[512,2560]{1,0:T(8,128)S(1)} %get-tuple-element.248) | copy-start | bytes 15728644 | tf_op jit(solution)/shard_map/while
  282.3 57.0 %all-to-all-start.1 = ((bf16[64,2,8192]{2,1,0:T(2,128)(2,1)}), bf16[64,2,8192]{2,1,0:T(2,128)(2,1)S(1)}, u32[]{:S(2)}, u32[]{:S(2)}) async-start(bf16[64,2,8192]{2,1,0:T(2,128)(2,1)} %reshape.225), calls=%async_computation.1 | async-start | bytes 4194304 | tf_op jit(solution)/shard_map/all_to_all | solution.py:81
  346.1 2.5 copy-start.4
  348.6 1.3 copy-start.2
Sparse Core Ops, SparseCore 0:
  41.7 97.4 all-gather.1
where the time goes:
time: 363 us; the launch traced here: 362 us
  waiting for transfers between devices  177 us (49%)
  local copies, waits for them, and re-layouts  59.8 us (16%)
  matrix products  40.7 us (11%)
  other arithmetic  35.6 us (10%)
  starting transfers between devices  21 us (6%)
  between operations  14.3 us (4%)
  loops' own time  13.4 us (4%)
    all_to_all x1, waiting for transfers between devices, local(): lax.all_to_all(payload, 'seq', split_axis=1, concat_axis=0, tiled=True)  126 us
    all_to_all x1, waiting for transfers between devices, local(): lax.all_to_all(back_rows.reshape(row_count_total, 1, HEAD_SIZE), 'seq', s...  50.6 us
    dot_general x5, matrix products, one_block(): jnp.dot(share, value_slots, preferred_element_type=jnp.float32)  24.1 us
    unnamed x15, local copies, waits for them, and re-layouts  17.2 us
    all_to_all x1, starting transfers between devices, local(): lax.all_to_all(payload, 'seq', split_axis=1, concat_axis=0, tiled=True)  15.1 us
    gather x1, local copies, waits for them, and re-layouts, local(): slot_docs = jnp.where(live, jnp.take(doc_ids[0], safe_tokens), -1)  13.8 us
    another operation x1, loops' own time, local(): mixed_blocks, stat_blocks = lax.map(one_block, starts)  13.4 us
    reduce_sum x5, other arithmetic, one_block(): totals = jnp.where(has_keys, jnp.sum(weights, axis=1), 1.0)  12.4 us
  transfers between devices with their start and end apart: 3, of which 2 were waited for; matrix products, arithmetic and copies ran while one was open for 32% of the time, Pallas kernels for 0%

commit v1 on v0

v1 whole, which is shorter than its diff:
```python
import functools
import math

import jax
import jax.numpy as jnp
from jax import lax
from jax.experimental import pallas as pl
from jax.experimental.pallas import tpu as pltpu
from jax.sharding import Mesh, PartitionSpec as P

HEAD_SIZE = 128
BLOCK = 128
BACK = 3
SCALE = 1.0 / math.sqrt(HEAD_SIZE)
SEQ = ("x", "z", "core")
VMEM = pltpu.CompilerParams(vmem_limit_bytes=48 * 1024 * 1024)


def attend_kernel(heads, kv_heads, head_of_ref, q_ref, bias_ref, kv3_ref, kv2_ref, kv1_ref, kv0_ref, mixed_ref, send_ref, lt_ref):
    per = heads // kv_heads
    width = kv_heads * HEAD_SIZE
    pieces = (kv3_ref, kv2_ref, kv1_ref, kv0_ref)
    bias = bias_ref[...]
    for g in range(kv_heads):
        at = g * HEAD_SIZE
        k = jnp.concatenate([p[:, at : at + HEAD_SIZE] for p in pieces], axis=0)
        v = jnp.concatenate([p[:, width + at : width + at + HEAD_SIZE] for p in pieces], axis=0)
        for h in range(g * per, (g + 1) * per):
            cols = slice(h * HEAD_SIZE, (h + 1) * HEAD_SIZE)
            s = lax.dot_general(k, q_ref[:, cols], (((1,), (1,)), ((), ())), preferred_element_type=jnp.float32)
            s = s + bias
            top = jnp.max(s, axis=0, keepdims=True)
            w = jnp.exp2((s - top) * (SCALE * math.log2(math.e)))
            total = jnp.sum(w, axis=0, keepdims=True)
            share = (w * (1.0 / total)).astype(jnp.bfloat16)
            mixed = lax.dot_general(v, share, (((0,), (0,)), ((), ())), preferred_element_type=jnp.float32)
            mixed_ref[:, cols] = mixed.T.astype(jnp.bfloat16)
            lt_ref[h : h + 1, :] = top * SCALE + jnp.log(total)
    for d in range(send_ref.shape[0]):
        send_ref[d : d + 1, :] = lt_ref[pl.ds(head_of_ref[d], 1), :]


def slots_kernel(got_ref, slot_ref, out_ref):
    slots = slot_ref[...]
    row = slots >> 7
    lane = slots & 127
    out = jnp.zeros(slots.shape, jnp.float32)
    for r in range(got_ref.shape[0]):
        source = jnp.broadcast_to(got_ref[r : r + 1, :], slots.shape)
        out = jnp.where(row == r, jnp.take_along_axis(source, lane, axis=1), out)
    out_ref[...] = out


def local(query, key_proj, value_projection_side, residual, w_out, doc_ids, slot_token, head_of):
    tok_rows = query.shape[1]
    heads = query.shape[2] // HEAD_SIZE
    kv_heads = key_proj.shape[2] // HEAD_SIZE
    seq_count = lax.axis_size(SEQ)
    me = lax.axis_index(SEQ)
    cores = lax.axis_size("core")
    part = w_out.shape[0] // cores
    w_part = lax.dynamic_slice_in_dim(w_out, lax.axis_index("core") * part, part, 0)
    w_all = lax.all_gather(w_part, ("fsdp", "core"), axis=0, tiled=True)

    kv = jnp.concatenate([key_proj[0], value_projection_side[0]], axis=1)
    before = [
        lax.ppermute(kv, SEQ, [(i, (i + back) % seq_count) for i in range(seq_count)])
        for back in range(1, BACK + 1)
    ]
    back_rows = BACK * tok_rows
    window = back_rows + tok_rows
    padded = jnp.concatenate([jnp.full((back_rows,), -1, jnp.int32), doc_ids[0]])
    docs = lax.dynamic_slice_in_dim(padded, me * tok_rows, window, 0)
    key_at = jnp.arange(window, dtype=jnp.int32)
    query_at = back_rows + jnp.arange(tok_rows, dtype=jnp.int32)
    allowed = (docs[:, None] == docs[None, back_rows:]) & (key_at[:, None] <= query_at[None, :])
    bias = jnp.where(allowed, 0.0, -1e30).astype(jnp.float32)

    whole = pl.BlockSpec(memory_space=pltpu.VMEM)
    mixed, send = pl.pallas_call(
        functools.partial(attend_kernel, heads, kv_heads),
        out_shape=(
            jax.ShapeDtypeStruct((tok_rows, heads * HEAD_SIZE), jnp.bfloat16),
            jax.ShapeDtypeStruct((seq_count, tok_rows), jnp.float32),
        ),
        in_specs=[pl.BlockSpec(memory_space=pltpu.SMEM)] + [whole] * 6,
        out_specs=(whole, whole),
        scratch_shapes=[pltpu.VMEM((heads, tok_rows), jnp.float32)],
        compiler_params=VMEM,
    )(head_of, query[0], bias, before[2], before[1], before[0], kv)

    got = lax.all_to_all(send, SEQ, split_axis=0, concat_axis=0, tiled=True)
    capacity = slot_token.shape[1]
    stats = pl.pallas_call(
        slots_kernel,
        out_shape=jax.ShapeDtypeStruct((capacity // 128, 128), jnp.float32),
        in_specs=[whole, whole],
        out_specs=whole,
        compiler_params=VMEM,
    )(got, slot_token.reshape(capacity // 128, 128))

    projected = jnp.dot(mixed, w_all, preferred_element_type=jnp.float32)
    layer_out = (residual[0].astype(jnp.float32) + projected).astype(jnp.bfloat16)[None]
    return (layer_out, stats.reshape(1, capacity))


def solution(mesh):
    split = Mesh(mesh.devices.reshape(4, 8, 2, 8), ("x", "z", "core", "fsdp"))
    return jax.shard_map(
        local,
        mesh=split,
        in_specs=(
            P("fsdp", SEQ, None),
            P("fsdp", SEQ, None),
            P("fsdp", SEQ, None),
            P("fsdp", SEQ, None),
            P("fsdp", None),
            P("fsdp", None),
            P("fsdp", SEQ),
            P(),
        ),
        out_specs=(P("fsdp", SEQ, None), P("fsdp", SEQ)),
        check_vma=False,
    )
```

time: 363 us -> 87.6 us (0.24)
  waiting for transfers between devices: 177 us -> 36.6 us
  local copies, waits for them, and re-layouts: 59.8 us -> 5.13 us
  matrix products: 40.7 us -> 5.49 us
  other arithmetic: 35.6 us -> 1.86 us
  loops' own time: 13.4 us -> 0 us
  Pallas kernels: 0 us -> 3.76 us
    all_to_all x2 -> x1, waiting for transfers between devices: 177 us -> 8.56 us  [local(): got = lax.all_to_all(send, SEQ, split_axis=0, concat_axis=0, tiled=True)]
    dot_general x12 -> x1, matrix products: 40.7 us -> 5.49 us  [local(): projected = jnp.dot(mixed, w_all, preferred_element_type=jnp.float32)]
    gather x5 -> x0, local copies, waits for them, and re-layouts: 29.5 us -> none  [the longest x1 13.8 us: local(): slot_docs = jnp.where(live, jnp.take(doc_ids[0], safe_tokens), -1)]
    ppermute x0 -> x3, waiting for transfers between devices: none -> 16.6 us  [local(): lax.ppermute(kv, SEQ, [(i, (i + back) % seq_count) for i in range(seq_cou...]
    all_to_all x2 -> x1, starting transfers between devices: 20.9 us -> 6.77 us  [local(): got = lax.all_to_all(send, SEQ, split_axis=0, concat_axis=0, tiled=True)]
    unnamed x15 -> x7, local copies, waits for them, and re-layouts: 17.2 us -> 3.51 us
    another operation x1 -> x0, loops' own time: 13.4 us -> none  [local(): mixed_blocks, stat_blocks = lax.map(one_block, starts)]
    ppermute x0 -> x3, starting transfers between devices: none -> 13.4 us  [local(): lax.ppermute(kv, SEQ, [(i, (i + back) % seq_count) for i in range(seq_cou...]
  transfers between devices with their start and end apart: 3 -> 5, of which waited for: 2 -> 4; matrix products, arithmetic and copies ran while one was open for 32% -> 4% of each run, Pallas kernels for 0% -> 4%
where the time goes in v1:
time: 87.6 us; the launch traced here: 87.2 us
  waiting for transfers between devices  36.6 us (42%)
  starting transfers between devices  20.2 us (23%)
  between operations  14.1 us (16%)
  matrix products  5.49 us (6%)
  local copies, waits for them, and re-layouts  5.13 us (6%)
  Pallas kernels  3.76 us (4%)
  other arithmetic  1.86 us (2%)
    ppermute x3, waiting for transfers between devices, local(): lax.ppermute(kv, SEQ, [(i, (i + back) % seq_count) for i in range(seq_cou...  16.6 us
    ppermute x3, starting transfers between devices, local(): lax.ppermute(kv, SEQ, [(i, (i + back) % seq_count) for i in range(seq_cou...  13.4 us
    all_gather x1, waiting for transfers between devices, local(): w_all = lax.all_gather(w_part, ('fsdp', 'core'), axis=0, tiled=True)  11.5 us
    all_to_all x1, waiting for transfers between devices, local(): got = lax.all_to_all(send, SEQ, split_axis=0, concat_axis=0, tiled=True)  8.56 us
    all_to_all x1, starting transfers between devices, local(): got = lax.all_to_all(send, SEQ, split_axis=0, concat_axis=0, tiled=True)  6.77 us
    dot_general x1, matrix products, local(): projected = jnp.dot(mixed, w_all, preferred_element_type=jnp.float32)  5.49 us
    unnamed x7, local copies, waits for them, and re-layouts  3.51 us
    pallas_call x1, Pallas kernels, local(): pl.pallas_call(functools.partial(attend_kernel, heads, kv_heads), out_sha...  3.22 us
  transfers between devices with their start and end apart: 5, of which 4 were waited for; matrix products, arithmetic and copies ran while one was open for 4% of the time, Pallas kernels for 4%

profile of v1, /device:TPU:1, one launch (start us, length us, event | category | flops | bytes accessed | tf_op | source)
XLA Modules:
  0.0 87.2 jit_solution(16335887078016198127)
XLA Ops:
  7.2 0.0 copy-start
  7.2 0.0 all-gather.2.cloned.1.call-start
  7.2 1.2 %copy-done = bf16[256,2048]{1,0:T(8,128)(2,1)S(1)} copy-done((bf16[256,2048]{1,0:T(8,128)(2,1)S(1)}, bf16[256,2048]{1,0:T(8,128)(2,1)}, u32[]{:S(2)}) %copy-start) | copy-done | bytes 1048600
  8.4 0.8 constant_dynamic-slice_fusion
  9.2 0.0 all-gather.2.cloned.1.call-update
  9.3 1.0 %pad_maximum_fusion.kv0_ref = bf16[128,1024]{1,0:T(8,128)(2,1)S(1)} fusion(bf16[128,512]{1,0:T(8,128)(2,1)} %bitcast.25, bf16[128,512]{1,0:T(8,128)(2,1)} %bitcast.26), kind=kLoop, calls=%fused_computation.3 | loop fusion | flops 524288 | bytes 524288 | tf_op jit(solution)/shard_map/concatenate | solution.py:65
  10.3 5.4 %collective-permute-start.2 = (bf16[128,1024]{1,0:T(8,128)(2,1)S(1)}, bf16[128,1024]{1,0:T(8,128)(2,1)S(1)}, u32[]{:S(2)}, u32[]{:S(2)}) collective-permute-start(bf16[128,1024]{1,0:T(8,128)(2,1)S(1)} %pad_maximum_fusion.kv0_ref), channel_id=1, source_target_pairs={{0,8},{8,16},{16,24},{24,32},{32,40},{40,48},{48,56},{56,64},{64,7... | collective-permute-start | bytes 786440 | tf_op jit(solution)/shard_map/ppermute | solution.py:67
  15.7 4.0 %collective-permute-start.1 = (bf16[128,1024]{1,0:T(8,128)(2,1)S(1)}, bf16[128,1024]{1,0:T(8,128)(2,1)S(1)}, u32[]{:S(2)}, u32[]{:S(2)}) collective-permute-start(bf16[128,1024]{1,0:T(8,128)(2,1)S(1)} %pad_maximum_fusion.kv0_ref), channel_id=1, source_target_pairs={{0,16},{8,24},{16,32},{24,40},{32,48},{40,56},{48,64},{56,72},{64,... | collective-permute-start | bytes 786440 | tf_op jit(solution)/shard_map/ppermute | solution.py:67
  19.7 4.0 %collective-permute-start = (bf16[128,1024]{1,0:T(8,128)(2,1)S(1)}, bf16[128,1024]{1,0:T(8,128)(2,1)S(1)}, u32[]{:S(2)}, u32[]{:S(2)}) collective-permute-start(bf16[128,1024]{1,0:T(8,128)(2,1)S(1)} %pad_maximum_fusion.kv0_ref), channel_id=1, source_target_pairs={{0,24},{8,32},{16,40},{24,48},{32,56},{40,64},{48,72},{56,80},{64,... | collective-permute-start | bytes 786440 | tf_op jit(solution)/shard_map/ppermute | solution.py:67
  23.7 0.8 pad_dynamic-slice_fusion
  24.5 0.1 fusion.3.bias_ref
  24.6 0.0 collective-permute-done.2.kv1_ref
  24.6 8.9 %collective-permute-done.1.kv2_ref = bf16[128,1024]{1,0:T(8,128)(2,1)S(1)} collective-permute-done((bf16[128,1024]{1,0:T(8,128)(2,1)S(1)}, bf16[128,1024]{1,0:T(8,128)(2,1)S(1)}, u32[]{:S(2)}, u32[]{:S(2)}) %collective-permute-start.1) | collective-permute-done | bytes 262176 | tf_op jit(solution)/shard_map/ppermute | solution.py:67
  33.6 7.7 %collective-permute-done.kv3_ref = bf16[128,1024]{1,0:T(8,128)(2,1)S(1)} collective-permute-done((bf16[128,1024]{1,0:T(8,128)(2,1)S(1)}, bf16[128,1024]{1,0:T(8,128)(2,1)S(1)}, u32[]{:S(2)}, u32[]{:S(2)}) %collective-permute-start) | collective-permute-done | bytes 262176 | tf_op jit(solution)/shard_map/ppermute | solution.py:67
  41.2 0.0 copy-start.1
  41.2 1.1 %copy-done.1 = bf16[1,128,2048]{2,1,0:T(8,128)(2,1)S(1)} copy-done((bf16[1,128,2048]{2,1,0:T(8,128)(2,1)S(1)}, bf16[1,128,2048]{2,1,0:T(8,128)(2,1)}, u32[]{:S(2)}) %copy-start.1) | copy-done | bytes 524312
  42.3 0.0 copy-start.2
  42.3 0.7 copy-done.2
  42.9 3.2 %shard_map.95 = (bf16[128,2048]{1,0:T(8,128)(2,1)S(1)}, f32[64,128]{1,0:T(8,128)}) custom-call(s32[64]{0:T(128)S(1)} %copy-done.2, bf16[128,2048]{1,0:T(8,128)(2,1)S(1)} %bitcast.21, f32[512,128]{1,0:T(8,128)S(1)} %fusion.3.bias_ref, bf16[128,1024]{1,0:T(8,128)(2,1)S(1)} %collective-permute-done.kv3_ref, ...), custom_call_target="tpu_custom_call" | custom-call | tf_op jit(solution)/shard_map/pallas_call | solution.py:80
  46.2 6.8 %all-to-all-start = ((f32[64,1,128]{2,1,0:T(1,128)}), f32[64,1,128]{2,1,0:T(1,128)S(1)}, u32[]{:S(2)}, u32[]{:S(2)}) async-start(f32[64,1,128]{2,1,0:T(1,128)} %bitcast.7), calls=%async_computation | async-start | bytes 65536 | tf_op jit(solution)/shard_map/all_to_all | solution.py:92
  52.9 0.7 reduce
  53.7 8.6 %all-to-all-done = f32[64,1,128]{2,1,0:T(1,128)S(1)} async-done(((f32[64,1,128]{2,1,0:T(1,128)}), f32[64,1,128]{2,1,0:T(1,128)S(1)}, u32[]{:S(2)}, u32[]{:S(2)}) %all-to-all-start) | async-done | bytes 32800 | tf_op jit(solution)/shard_map/all_to_all | solution.py:92
  62.2 0.5 shard_map.96
  62.8 0.6 copy.13
  63.4 11.5 %all-gather.2.cloned.1.call-done = bf16[2048,2048]{1,0:T(8,128)(2,1)} async-done(((bf16[128,2048]{1,0:T(8,128)(2,1)}), bf16[2048,2048]{1,0:T(8,128)(2,1)}) %all-gather.2.cloned.1.call-update) | async-done | bytes 8388624 | tf_op jit(solution)/shard_map/all_gather | solution.py:63
  74.9 5.5 %fusion.1 = bf16[1,128,2048]{2,1,0:T(8,128)(2,1)} fusion(bf16[128,2048]{1,0:T(8,128)(2,1)S(1)} %get-tuple-element.4, bf16[2048,2048]{1,0:T(8,128)(2,1)} %all-gather.2.cloned.1.call-done, bf16[1,128,2048]{2,1,0:T(8,128)(2,1)} %param.11), kind=kOutput, calls=%fused_computation.2 | convolution fusion | flops 1074528256 | bytes 9961472 | tf_op jit(solution)/shard_map/dot_general | solution.py:102
  (2 shorter events, 0.0 us)
Async XLA Ops:
  7.2 1.2 %copy-start = (bf16[256,2048]{1,0:T(8,128)(2,1)S(1)}, bf16[256,2048]{1,0:T(8,128)(2,1)}, u32[]{:S(2)}) copy-start(bf16[256,2048]{1,0:T(8,128)(2,1)} %param.12) | copy-start | bytes 3145732
  7.2 67.7 %all-gather.2.cloned.1.call-start = ((), (), s32[]{:S(2)}) async-start(), calls=%async_computation.1 | async-start | bytes 8912896 | tf_op jit(solution)/shard_map/all_gather | solution.py:63
  10.3 14.4 %collective-permute-start.2 = (bf16[128,1024]{1,0:T(8,128)(2,1)S(1)}, bf16[128,1024]{1,0:T(8,128)(2,1)S(1)}, u32[]{:S(2)}, u32[]{:S(2)}) collective-permute-start(bf16[128,1024]{1,0:T(8,128)(2,1)S(1)} %pad_maximum_fusion.kv0_ref), channel_id=1, source_target_pairs={{0,8},{8,16},{16,24},{24,32},{32,40},{40,48},{48,56},{56,64},{64,7... | collective-permute-start | bytes 786440 | tf_op jit(solution)/shard_map/ppermute | solution.py:67
  15.7 17.9 %collective-permute-start.1 = (bf16[128,1024]{1,0:T(8,128)(2,1)S(1)}, bf16[128,1024]{1,0:T(8,128)(2,1)S(1)}, u32[]{:S(2)}, u32[]{:S(2)}) collective-permute-start(bf16[128,1024]{1,0:T(8,128)(2,1)S(1)} %pad_maximum_fusion.kv0_ref), channel_id=1, source_target_pairs={{0,16},{8,24},{16,32},{24,40},{32,48},{40,56},{48,64},{56,72},{64,... | collective-permute-start | bytes 786440 | tf_op jit(solution)/shard_map/ppermute | solution.py:67
  19.7 21.6 %collective-permute-start = (bf16[128,1024]{1,0:T(8,128)(2,1)S(1)}, bf16[128,1024]{1,0:T(8,128)(2,1)S(1)}, u32[]{:S(2)}, u32[]{:S(2)}) collective-permute-start(bf16[128,1024]{1,0:T(8,128)(2,1)S(1)} %pad_maximum_fusion.kv0_ref), channel_id=1, source_target_pairs={{0,24},{8,32},{16,40},{24,48},{32,56},{40,64},{48,72},{56,80},{64,... | collective-permute-start | bytes 786440 | tf_op jit(solution)/shard_map/ppermute | solution.py:67
  41.2 1.1 %copy-start.1 = (bf16[1,128,2048]{2,1,0:T(8,128)(2,1)S(1)}, bf16[1,128,2048]{2,1,0:T(8,128)(2,1)}, u32[]{:S(2)}) copy-start(bf16[1,128,2048]{2,1,0:T(8,128)(2,1)} %param.8) | copy-start | bytes 1572868
  42.3 0.7 copy-start.2
  46.2 16.1 %all-to-all-start = ((f32[64,1,128]{2,1,0:T(1,128)}), f32[64,1,128]{2,1,0:T(1,128)S(1)}, u32[]{:S(2)}, u32[]{:S(2)}) async-start(f32[64,1,128]{2,1,0:T(1,128)} %bitcast.7), calls=%async_computation | async-start | bytes 65536 | tf_op jit(solution)/shard_map/all_to_all | solution.py:92
Sparse Core Ops, SparseCore 0:
  10.7 64.1 all-gather.1

commit v2 on v1

--- a/solution.py
+++ b/solution.py
@@ -13,13 +13,14 @@
 BACK = 3
 SCALE = 1.0 / math.sqrt(HEAD_SIZE)
 SEQ = ("x", "z", "core")
-VMEM = pltpu.CompilerParams(vmem_limit_bytes=48 * 1024 * 1024)
-
-
-def attend_kernel(heads, kv_heads, head_of_ref, q_ref, bias_ref, kv3_ref, kv2_ref, kv1_ref, kv0_ref, mixed_ref, send_ref, lt_ref):
+VMEM = pltpu.CompilerParams(vmem_limit_bytes=14 * 1024 * 1024)
+STREAM = pltpu.CompilerParams(vmem_limit_bytes=56 * 1024 * 1024)
+
+
+def attend_kernel(heads, kv_heads, head_of_ref, q_ref, bias_ref, kv0_ref, kv1_ref, kv2_ref, kv3_ref, mixed_ref, send_ref, lt_ref):
     per = heads // kv_heads
     width = kv_heads * HEAD_SIZE
-    pieces = (kv3_ref, kv2_ref, kv1_ref, kv0_ref)
+    pieces = (kv0_ref, kv1_ref, kv2_ref, kv3_ref)
     bias = bias_ref[...]
     for g in range(kv_heads):
         at = g * HEAD_SIZE
@@ -51,44 +52,110 @@
     out_ref[...] = out
 
 
+def streamed(tokens_ref, weight_ref, held_ref, rows_ref, sems):
+    count = sems.shape[0] - 1
+    step = weight_ref.shape[0] // count
+    parts = [pl.ds(i * step, step) for i in range(count)]
+    tokens = pltpu.make_async_copy(tokens_ref, rows_ref, sems.at[count])
+    copies = [pltpu.make_async_copy(weight_ref.at[p], held_ref.at[p], sems.at[i]) for i, p in enumerate(parts)]
+    tokens.start()
+    for copy in copies:
+        copy.start()
+    tokens.wait()
+    total = None
+    for copy, part in zip(copies, parts):
+        copy.wait()
+        product = jnp.dot(rows_ref[:, part], held_ref[part, :], preferred_element_type=jnp.float32)
+        total = product if total is None else total + product
+    return total
+
+
+def away_kernel(tokens_ref, weight_ref, out_ref, held_ref, rows_ref, sems):
+    out_ref[...] = streamed(tokens_ref, weight_ref, held_ref, rows_ref, sems).astype(jnp.bfloat16)
+
+
+def here_kernel(side_ref, tokens_ref, weight_ref, residual_ref, out_ref, held_ref, rows_ref, sems, half_ref, sem):
+    width = half_ref.shape[1]
+    mine = pl.ds(pl.multiple_of(side_ref[0] * width, width), width)
+    total = streamed(tokens_ref, weight_ref, held_ref, rows_ref, sems)
+    half_ref[...] = (residual_ref[:, mine].astype(jnp.float32) + total).astype(jnp.bfloat16)
+    copy = pltpu.make_async_copy(half_ref, out_ref.at[:, mine], sem)
+    copy.start()
+    copy.wait()
+
+
+def join_kernel(side_ref, here_ref, back_ref, residual_ref, out_ref, half_ref, sem):
+    width = half_ref.shape[1]
+    theirs = pl.ds(pl.multiple_of((1 - side_ref[0]) * width, width), width)
+    total = residual_ref[:, theirs].astype(jnp.float32) + back_ref[...].astype(jnp.float32)
+    half_ref[...] = total.astype(jnp.bfloat16)
+    copy = pltpu.make_async_copy(half_ref, out_ref.at[:, theirs], sem)
+    copy.start()
+    copy.wait()
+
+
+def after(x, *others):
+    anywhere = pl.BlockSpec(memory_space=pl.ANY)
+    return pl.pallas_call(
+        lambda *refs: None,
+        out_shape=jax.ShapeDtypeStruct(x.shape, x.dtype),
+        in_specs=[anywhere] * (1 + len(others)),
+        out_specs=anywhere,
+        input_output_aliases={0: 0},
+        compiler_params=pltpu.CompilerParams(vmem_limit_bytes=1024 * 1024),
+    )(x, *others)
+
+
 def local(query, key_proj, value_projection_side, residual, w_out, doc_ids, slot_token, head_of):
     tok_rows = query.shape[1]
     heads = query.shape[2] // HEAD_SIZE
     kv_heads = key_proj.shape[2] // HEAD_SIZE
     seq_count = lax.axis_size(SEQ)
     me = lax.axis_index(SEQ)
-    cores = lax.axis_size("core")
-    part = w_out.shape[0] // cores
-    w_part = lax.dynamic_slice_in_dim(w_out, lax.axis_index("core") * part, part, 0)
-    w_all = lax.all_gather(w_part, ("fsdp", "core"), axis=0, tiled=True)
+    core = lax.axis_index("core")
+    side = lax.axis_index("x") % 2
+    half = w_out.shape[0] // 2
+    columns = w_out.shape[1]
+    width = columns // 2
+    swap = [(i, i ^ 1) for i in range(seq_count)]
+    pair = [(i, i ^ 1) for i in range(lax.axis_size("x"))]
+
+    anywhere = pl.BlockSpec(memory_space=pl.ANY)
+    whole = pl.BlockSpec(memory_space=pltpu.VMEM)
+    scalars = pl.BlockSpec(memory_space=pltpu.SMEM)
+    part = lax.dynamic_slice(w_out, (core * half, side * width), (half, width))
+    weight = lax.all_gather(part, ("fsdp", "core"), axis=0, tiled=True)
 
     kv = jnp.concatenate([key_proj[0], value_projection_side[0]], axis=1)
-    before = [
-        lax.ppermute(kv, SEQ, [(i, (i + back) % seq_count) for i in range(seq_count)])
-        for back in range(1, BACK + 1)
-    ]
+    kv1 = lax.ppermute(kv, SEQ, [(i, (i + 2) % seq_count) for i in range(seq_count)])
+    kv2 = lax.ppermute(kv, SEQ, [(i, (i + (3 if i % 2 else 1)) % seq_count) for i in range(seq_count)])
+    kv3 = lax.ppermute(kv1, SEQ, swap)
+
     back_rows = BACK * tok_rows
-    window = back_rows + tok_rows
     padded = jnp.concatenate([jnp.full((back_rows,), -1, jnp.int32), doc_ids[0]])
-    docs = lax.dynamic_slice_in_dim(padded, me * tok_rows, window, 0)
-    key_at = jnp.arange(window, dtype=jnp.int32)
-    query_at = back_rows + jnp.arange(tok_rows, dtype=jnp.int32)
-    allowed = (docs[:, None] == docs[None, back_rows:]) & (key_at[:, None] <= query_at[None, :])
+    behind = (0, 2, 3 - 2 * core, 1 + 2 * core)
+    query_docs = lax.dynamic_slice_in_dim(padded, (me + BACK) * tok_rows, tok_rows, 0)
+    docs = jnp.concatenate([lax.dynamic_slice_in_dim(padded, (me + BACK - b) * tok_rows, tok_rows, 0) for b in behind])
+    key_at = jnp.arange((BACK + 1) * tok_rows, dtype=jnp.int32)
+    query_at = jnp.arange(tok_rows, dtype=jnp.int32)
+    allowed = (docs[:, None] == query_docs[None, :]) & (
+        (key_at[:, None] >= tok_rows) | (key_at[:, None] <= query_at[None, :])
+    )
     bias = jnp.where(allowed, 0.0, -1e30).astype(jnp.float32)
 
-    whole = pl.BlockSpec(memory_space=pltpu.VMEM)
     mixed, send = pl.pallas_call(
         functools.partial(attend_kernel, heads, kv_heads),
         out_shape=(
             jax.ShapeDtypeStruct((tok_rows, heads * HEAD_SIZE), jnp.bfloat16),
             jax.ShapeDtypeStruct((seq_count, tok_rows), jnp.float32),
         ),
-        in_specs=[pl.BlockSpec(memory_space=pltpu.SMEM)] + [whole] * 6,
+        in_specs=[scalars] + [whole] * 6,
         out_specs=(whole, whole),
         scratch_shapes=[pltpu.VMEM((heads, tok_rows), jnp.float32)],
         compiler_params=VMEM,
-    )(head_of, query[0], bias, before[2], before[1], before[0], kv)
-
+    )(head_of, query[0], bias, kv, kv1, kv2, kv3)
+
+    theirs = lax.ppermute(mixed, "x", pair)
     got = lax.all_to_all(send, SEQ, split_axis=0, concat_axis=0, tiled=True)
     capacity = slot_token.shape[1]
     stats = pl.pallas_call(
@@ -98,10 +165,42 @@
         out_specs=whole,
         compiler_params=VMEM,
     )(got, slot_token.reshape(capacity // 128, 128))
-
-    projected = jnp.dot(mixed, w_all, preferred_element_type=jnp.float32)
-    layer_out = (residual[0].astype(jnp.float32) + projected).astype(jnp.bfloat16)[None]
-    return (layer_out, stats.reshape(1, capacity))
+    theirs = after(theirs, got)
+    scratch = [
+        pltpu.VMEM((columns, width), jnp.bfloat16),
+        pltpu.VMEM((tok_rows, columns), jnp.bfloat16),
+        pltpu.SemaphoreType.DMA((9,)),
+    ]
+    half_scratch = [pltpu.VMEM((tok_rows, width), jnp.bfloat16), pltpu.SemaphoreType.DMA]
+    away = pl.pallas_call(
+        away_kernel,
+        out_shape=jax.ShapeDtypeStruct((tok_rows, width), jnp.bfloat16),
+        in_specs=[anywhere, anywhere],
+        out_specs=whole,
+        scratch_shapes=scratch,
+        compiler_params=STREAM,
+    )(theirs, weight)
+    back = lax.ppermute(away, "x", pair)
+    result = jax.ShapeDtypeStruct((tok_rows, columns), jnp.bfloat16)
+    side = side[None].astype(jnp.int32)
+    here = pl.pallas_call(
+        here_kernel,
+        out_shape=result,
+        in_specs=[scalars, anywhere, anywhere, whole],
+        out_specs=anywhere,
+        scratch_shapes=scratch + half_scratch,
+        compiler_params=STREAM,
+    )(side, mixed, weight, residual[0])
+    layer_out = pl.pallas_call(
+        join_kernel,
+        out_shape=result,
+        in_specs=[scalars, anywhere, whole, whole],
+        out_specs=anywhere,
+        scratch_shapes=half_scratch,
+        input_output_aliases={1: 0},
+        compiler_params=VMEM,
+    )(side, here, back, residual[0])
+    return (layer_out[None], stats.reshape(1, capacity))
 
 
 def solution(mesh):

time: 87.6 us -> 82.1 us (0.937)
  waiting for transfers between devices: 36.6 us -> 11.2 us
  blocking collectives: 0 us -> 16.6 us
  Pallas kernels: 3.76 us -> 11.9 us
  matrix products: 5.49 us -> 0 us
    all_to_all x0 -> x1, blocking collectives: none -> 16.6 us  [local(): got = lax.all_to_all(send, SEQ, split_axis=0, concat_axis=0, tiled=True)]
    all_gather x1, waiting for transfers between devices: 11.5 us -> 1.77 us  [local(): weight = lax.all_gather(part, ('fsdp', 'core'), axis=0, tiled=True)]
    all_to_all x1 -> x0, waiting for transfers between devices: 8.56 us -> none  [local(): got = lax.all_to_all(send, SEQ, split_axis=0, concat_axis=0, tiled=True)]
    pallas_call x0 -> x4, Pallas kernels: none -> 8.47 us  [the longest x1 4.37 us: local(): pl.pallas_call(here_kernel, out_shape=result, in_specs=[scalars, anywhere...]
    ppermute x3 -> x5, starting transfers between devices: 13.4 us -> 20.6 us  [the longest x1 6.65 us: local(): lax.ppermute(kv, SEQ, [(i, (i + (3 if i % 2 else 1)) % seq_count) for i i...]
    ppermute x3 -> x5, waiting for transfers between devices: 16.6 us -> 9.45 us  [the longest x1 7.25 us: local(): lax.ppermute(kv, SEQ, [(i, (i + 2) % seq_count) for i in range(seq_count)])]
    all_to_all x1 -> x0, starting transfers between devices: 6.77 us -> none  [local(): got = lax.all_to_all(send, SEQ, split_axis=0, concat_axis=0, tiled=True)]
    dot_general x1 -> x0, matrix products: 5.49 us -> none  [local(): projected = jnp.dot(mixed, w_all, preferred_element_type=jnp.float32)]
  transfers between devices with their start and end apart: 5 -> 6, of which waited for: 4 -> 4; matrix products, arithmetic and copies ran while one was open for 4% -> 3% of each run, Pallas kernels for 4% -> 10%
where the time goes in v2:
time: 82.1 us; the launch traced here: 81.6 us
  starting transfers between devices  20.6 us (25%)
  blocking collectives  16.6 us (20%)
  between operations  14.2 us (17%)
  Pallas kernels  11.9 us (14%)
  waiting for transfers between devices  11.2 us (14%)
  local copies, waits for them, and re-layouts  5.76 us (7%)
  other arithmetic  1.24 us (2%)
    all_to_all x1, blocking collectives, local(): got = lax.all_to_all(send, SEQ, split_axis=0, concat_axis=0, tiled=True)  16.6 us
    ppermute x1, waiting for transfers between devices, local(): lax.ppermute(kv, SEQ, [(i, (i + 2) % seq_count) for i in range(seq_count)])  7.25 us
    ppermute x1, starting transfers between devices, local(): lax.ppermute(kv, SEQ, [(i, (i + (3 if i % 2 else 1)) % seq_count) for i i...  6.65 us
    ppermute x1, starting transfers between devices, local(): lax.ppermute(kv, SEQ, [(i, (i + 2) % seq_count) for i in range(seq_count)])  4.83 us
    pallas_call x1, Pallas kernels, local(): pl.pallas_call(here_kernel, out_shape=result, in_specs=[scalars, anywhere...  4.37 us
    ppermute x1, starting transfers between devices, local(): kv3 = lax.ppermute(kv1, SEQ, swap)  4.34 us
    pallas_call x1, Pallas kernels, local(): pl.pallas_call(away_kernel, out_shape=jax.ShapeDtypeStruct((tok_rows, wid...  3.33 us
    unnamed x13, local copies, waits for them, and re-layouts  3.13 us
  transfers between devices with their start and end apart: 6, of which 4 were waited for; matrix products, arithmetic and copies ran while one was open for 3% of the time, Pallas kernels for 10%

profile of v2, /device:TPU:1, one launch (start us, length us, event | category | flops | bytes accessed | tf_op | source)
XLA Modules:
  0.0 81.6 jit_solution(745294043580451486)
XLA Ops:
  7.2 0.0 all-gather.2.cloned.1.call-start
  7.2 1.7 %dynamic_slice.20 = bf16[128,1024]{1,0:T(8,128)(2,1)} dynamic-slice(bf16[256,2048]{1,0:T(8,128)(2,1)} %param.12, s32[]{:T(128)S(6)} %select_n.36, s32[]{:T(128)S(6)} %select_n.37), dynamic_slice_sizes={128,1024} | dynamic-slice | bytes 524292 | tf_op jit(solution)/shard_map/dynamic_slice | solution.py:126
  8.9 0.0 all-gather.2.cloned.1.call-update
  8.9 1.0 %pad_maximum_fusion.kv0_ref = bf16[128,1024]{1,0:T(8,128)(2,1)S(1)} fusion(bf16[128,512]{1,0:T(8,128)(2,1)} %bitcast.26, bf16[128,512]{1,0:T(8,128)(2,1)} %bitcast.27), kind=kLoop, calls=%fused_computation | loop fusion | flops 524288 | bytes 524288 | tf_op jit(solution)/shard_map/concatenate | solution.py:129
  9.9 0.0 copy-start.5
  9.9 4.8 %collective-permute-start = (bf16[128,1024]{1,0:T(8,128)(2,1)S(1)}, bf16[128,1024]{1,0:T(8,128)(2,1)S(1)}, u32[]{:S(2)}, u32[]{:S(2)}) collective-permute-start(bf16[128,1024]{1,0:T(8,128)(2,1)S(1)} %pad_maximum_fusion.kv0_ref), channel_id=1, source_target_pairs={{0,16},{8,24},{16,32},{24,40},{32,48},{40,56},{48,64},{56,72},{64,... | collective-permute-start | bytes 786440 | tf_op jit(solution)/shard_map/ppermute | solution.py:130
  14.8 6.6 %collective-permute-start.1 = (bf16[128,1024]{1,0:T(8,128)(2,1)S(1)}, bf16[128,1024]{1,0:T(8,128)(2,1)S(1)}, u32[]{:S(2)}, u32[]{:S(2)}) collective-permute-start(bf16[128,1024]{1,0:T(8,128)(2,1)S(1)} %pad_maximum_fusion.kv0_ref), channel_id=1, source_target_pairs={{0,8},{8,32},{16,24},{24,48},{32,40},{40,64},{48,56},{56,80},{64,7... | collective-permute-start | bytes 786440 | tf_op jit(solution)/shard_map/ppermute | solution.py:131
  21.5 0.9 %pad_dynamic-slice_fusion.2 = (s32[128]{0:T(128)S(1)}, s32[128]{0:T(128)S(1)}, s32[128]{0:T(128)S(1)}, s32[128]{0:T(128)S(1)}) fusion(s32[]{:T(128)S(6)} %select_n.32, s32[8192]{0:T(1024)} %bitcast.28, s32[]{:T(128)S(6)} %select_n.33, s32[]{:T(128)S(6)} %select_n.34, s32[]{:T(128)S(6)} %select_n.31), kind=kLoop, calls=%fused_computation.7 | loop fusion | bytes 34832 | tf_op jit(solution)/shard_map/dynamic_slice | solution.py:138
  22.4 7.2 %collective-permute-done.kv1_ref = bf16[128,1024]{1,0:T(8,128)(2,1)S(1)} collective-permute-done((bf16[128,1024]{1,0:T(8,128)(2,1)S(1)}, bf16[128,1024]{1,0:T(8,128)(2,1)S(1)}, u32[]{:S(2)}, u32[]{:S(2)}) %collective-permute-start) | collective-permute-done | bytes 262176 | tf_op jit(solution)/shard_map/ppermute | solution.py:130
  29.7 4.3 %collective-permute-start.2 = (bf16[128,1024]{1,0:T(8,128)(2,1)S(1)}, bf16[128,1024]{1,0:T(8,128)(2,1)S(1)}, u32[]{:S(2)}, u32[]{:S(2)}) collective-permute-start(bf16[128,1024]{1,0:T(8,128)(2,1)S(1)} %collective-permute-done.kv1_ref), channel_id=1, source_target_pairs={{0,8},{8,0},{16,24},{24,16},{32,40},{40,32},{48,56},{56,48},{64,72... | collective-permute-start | bytes 786440 | tf_op jit(solution)/shard_map/ppermute | solution.py:132
  34.0 0.2 fusion.2.bias_ref
  34.2 0.0 collective-permute-done.1.kv2_ref
  34.2 0.9 %collective-permute-done.2.kv3_ref = bf16[128,1024]{1,0:T(8,128)(2,1)S(1)} collective-permute-done((bf16[128,1024]{1,0:T(8,128)(2,1)S(1)}, bf16[128,1024]{1,0:T(8,128)(2,1)S(1)}, u32[]{:S(2)}, u32[]{:S(2)}) %collective-permute-start.2) | collective-permute-done | bytes 262176 | tf_op jit(solution)/shard_map/ppermute | solution.py:132
  35.2 0.0 copy-start.3
  35.2 1.0 %copy-done.3 = bf16[1,128,2048]{2,1,0:T(8,128)(2,1)S(1)} copy-done((bf16[1,128,2048]{2,1,0:T(8,128)(2,1)S(1)}, bf16[1,128,2048]{2,1,0:T(8,128)(2,1)}, u32[]{:S(2)}) %copy-start.3) | copy-done | bytes 524312
  36.2 0.0 copy-start.4
  36.2 0.7 copy-done.4
  36.9 2.9 %shard_map.95 = (bf16[128,2048]{1,0:T(8,128)(2,1)S(1)}, f32[64,128]{1,0:T(8,128)S(1)}) custom-call(s32[64]{0:T(128)S(1)} %copy-done.4, bf16[128,2048]{1,0:T(8,128)(2,1)S(1)} %bitcast.19, f32[512,128]{1,0:T(8,128)S(1)} %fusion.2.bias_ref, bf16[128,1024]{1,0:T(8,128)(2,1)S(1)} %pad_maximum_fusion.kv0_ref, bf16[128,1024]{1,0:T(8,128)(2,1)S(1)} %collective-permute-done.kv1_ref, ...), custom_call_target="tpu_custom_call" | custom-call | tf_op jit(solution)/shard_map/pallas_call | solution.py:146
  39.7 0.0 copy-start.2
  39.7 1.9 %collective-permute-start.3 = (bf16[128,2048]{1,0:T(8,128)(2,1)S(1)}, bf16[128,2048]{1,0:T(8,128)(2,1)S(1)}, u32[]{:S(2)}, u32[]{:S(2)}) collective-permute-start(bf16[128,2048]{1,0:T(8,128)(2,1)S(1)} %get-tuple-element.4.tokens_ref), channel_id=1, source_target_pairs={{0,128},{128,0},{256,384},{384,256},{1,129},{129,1},{257,385},{385... | collective-permute-start | bytes 1572872 | tf_op jit(solution)/shard_map/ppermute | solution.py:158
  41.7 16.6 %all_to_all.11 = f32[64,1,128]{2,1,0:T(1,128)S(1)} all-to-all(f32[64,1,128]{2,1,0:T(1,128)S(1)} %bitcast.24), channel_id=1, replica_groups=mesh['x'=4,'z'=8,'core'=2,'fsdp'=8] {'x','z','core'}, dimensions={0} | all-to-all | bytes 65536 | tf_op jit(solution)/shard_map/all_to_all | solution.py:159
  58.3 0.0 collective-permute-done.3.refs_0_
  58.3 0.0 copy-start
  58.3 0.8 copy-done
  59.1 0.0 copy-start.1
  59.1 1.8 %all-gather.2.cloned.1.call-done.weight_ref = bf16[2048,1024]{1,0:T(8,128)(2,1)} async-done(((bf16[128,1024]{1,0:T(8,128)(2,1)}), bf16[2048,1024]{1,0:T(8,128)(2,1)}) %all-gather.2.cloned.1.call-update) | async-done | bytes 4194320 | tf_op jit(solution)/shard_map/all_gather | solution.py:127
  60.9 3.3 %shard_map.98 = bf16[128,1024]{1,0:T(8,128)(2,1)} custom-call(bf16[128,2048]{1,0:T(8,128)(2,1)} %copy-done, bf16[2048,1024]{1,0:T(8,128)(2,1)} %all-gather.2.cloned.1.call-done.weight_ref), custom_call_target="tpu_custom_call" | custom-call | tf_op jit(solution)/shard_map/pallas_call | solution.py:175
  64.2 2.9 %collective-permute-start.4 = (bf16[128,1024]{1,0:T(8,128)(2,1)}, bf16[128,1024]{1,0:T(8,128)(2,1)S(1)}, u32[]{:S(2)}, u32[]{:S(2)}) collective-permute-start(bf16[128,1024]{1,0:T(8,128)(2,1)} %shard_map.98), channel_id=1, source_target_pairs={{0,128},{128,0},{256,384},{384,256},{1,129},{129,1},{257,385},{385... | collective-permute-start | bytes 786440 | tf_op jit(solution)/shard_map/ppermute | solution.py:183
  67.1 0.0 copy-done.5
  67.1 0.5 shard_map.100
  67.7 0.6 copy.15
  68.3 0.0 copy-done.2
  68.3 4.4 %shard_map.96.here_ref = bf16[128,2048]{1,0:T(8,128)(2,1)} custom-call(s32[1]{0:T(128)} %bitcast.side_ref, bf16[128,2048]{1,0:T(8,128)(2,1)} %copy-done.2, bf16[2048,1024]{1,0:T(8,128)(2,1)} %all-gather.2.cloned.1.call-done.weight_ref, bf16[128,2048]{1,0:T(8,128)(2,1)} %bitcast.17), custom_call_target="tpu_custom_call" | custom-call | tf_op jit(solution)/shard_map/pallas_call | solution.py:186
  72.7 1.3 %collective-permute-done.4.back_ref = bf16[128,1024]{1,0:T(8,128)(2,1)S(1)} collective-permute-done((bf16[128,1024]{1,0:T(8,128)(2,1)}, bf16[128,1024]{1,0:T(8,128)(2,1)S(1)}, u32[]{:S(2)}, u32[]{:S(2)}) %collective-permute-start.4) | collective-permute-done | bytes 262176 | tf_op jit(solution)/shard_map/ppermute | solution.py:183
  74.0 0.0 copy-done.1
  74.0 0.8 shard_map.99
  (4 shorter events, 0.0 us)
Async XLA Ops:
  7.2 53.7 %all-gather.2.cloned.1.call-start = ((), (), s32[]{:S(2)}) async-start(), calls=%async_computation.1 | async-start | bytes 4456448 | tf_op jit(solution)/shard_map/all_gather | solution.py:127
  9.9 57.2 %copy-start.5 = (s32[1,2560]{1,0:T(1,128)S(1)}, s32[1,2560]{1,0:T(1,128)}, u32[]{:S(2)}) copy-start(s32[1,2560]{1,0:T(1,128)} %param.14) | copy-start | bytes 30724
  9.9 19.7 %collective-permute-start = (bf16[128,1024]{1,0:T(8,128)(2,1)S(1)}, bf16[128,1024]{1,0:T(8,128)(2,1)S(1)}, u32[]{:S(2)}, u32[]{:S(2)}) collective-permute-start(bf16[128,1024]{1,0:T(8,128)(2,1)S(1)} %pad_maximum_fusion.kv0_ref), channel_id=1, source_target_pairs={{0,16},{8,24},{16,32},{24,40},{32,48},{40,56},{48,64},{56,72},{64,... | collective-permute-start | bytes 786440 | tf_op jit(solution)/shard_map/ppermute | solution.py:130
  14.8 19.5 %collective-permute-start.1 = (bf16[128,1024]{1,0:T(8,128)(2,1)S(1)}, bf16[128,1024]{1,0:T(8,128)(2,1)S(1)}, u32[]{:S(2)}, u32[]{:S(2)}) collective-permute-start(bf16[128,1024]{1,0:T(8,128)(2,1)S(1)} %pad_maximum_fusion.kv0_ref), channel_id=1, source_target_pairs={{0,8},{8,32},{16,24},{24,48},{32,40},{40,64},{48,56},{56,80},{64,7... | collective-permute-start | bytes 786440 | tf_op jit(solution)/shard_map/ppermute | solution.py:131
  29.7 5.5 %collective-permute-start.2 = (bf16[128,1024]{1,0:T(8,128)(2,1)S(1)}, bf16[128,1024]{1,0:T(8,128)(2,1)S(1)}, u32[]{:S(2)}, u32[]{:S(2)}) collective-permute-start(bf16[128,1024]{1,0:T(8,128)(2,1)S(1)} %collective-permute-done.kv1_ref), channel_id=1, source_target_pairs={{0,8},{8,0},{16,24},{24,16},{32,40},{40,32},{48,56},{56,48},{64,72... | collective-permute-start | bytes 786440 | tf_op jit(solution)/shard_map/ppermute | solution.py:132
  35.2 1.0 %copy-start.3 = (bf16[1,128,2048]{2,1,0:T(8,128)(2,1)S(1)}, bf16[1,128,2048]{2,1,0:T(8,128)(2,1)}, u32[]{:S(2)}) copy-start(bf16[1,128,2048]{2,1,0:T(8,128)(2,1)} %param.8) | copy-start | bytes 1572868
  36.2 0.7 copy-start.4
  39.7 28.6 %copy-start.2 = (bf16[128,2048]{1,0:T(8,128)(2,1)}, bf16[128,2048]{1,0:T(8,128)(2,1)S(1)}, u32[]{:S(2)}) copy-start(bf16[128,2048]{1,0:T(8,128)(2,1)S(1)} %get-tuple-element.4.tokens_ref) | copy-start | bytes 1572868
  39.7 18.6 %collective-permute-start.3 = (bf16[128,2048]{1,0:T(8,128)(2,1)S(1)}, bf16[128,2048]{1,0:T(8,128)(2,1)S(1)}, u32[]{:S(2)}, u32[]{:S(2)}) collective-permute-start(bf16[128,2048]{1,0:T(8,128)(2,1)S(1)} %get-tuple-element.4.tokens_ref), channel_id=1, source_target_pairs={{0,128},{128,0},{256,384},{384,256},{1,129},{129,1},{257,385},{385... | collective-permute-start | bytes 1572872 | tf_op jit(solution)/shard_map/ppermute | solution.py:158
  58.3 0.8 copy-start
  59.1 14.9 %copy-start.1 = (bf16[1,128,2048]{2,1,0:T(8,128)(2,1)S(1)}, bf16[1,128,2048]{2,1,0:T(8,128)(2,1)}, u32[]{:S(2)}) copy-start(bf16[1,128,2048]{2,1,0:T(8,128)(2,1)} %param.11) | copy-start | bytes 1572868
  64.2 9.8 %collective-permute-start.4 = (bf16[128,1024]{1,0:T(8,128)(2,1)}, bf16[128,1024]{1,0:T(8,128)(2,1)S(1)}, u32[]{:S(2)}, u32[]{:S(2)}) collective-permute-start(bf16[128,1024]{1,0:T(8,128)(2,1)} %shard_map.98), channel_id=1, source_target_pairs={{0,128},{128,0},{256,384},{384,256},{1,129},{129,1},{257,385},{385... | collective-permute-start | bytes 786440 | tf_op jit(solution)/shard_map/ppermute | solution.py:183
Sparse Core Ops, SparseCore 0:
  10.1 50.7 all-gather.1

commit v3 on v2

--- a/solution.py
+++ b/solution.py
@@ -49,7 +49,8 @@
     for r in range(got_ref.shape[0]):
         source = jnp.broadcast_to(got_ref[r : r + 1, :], slots.shape)
         out = jnp.where(row == r, jnp.take_along_axis(source, lane, axis=1), out)
-    out_ref[...] = out
+    for r in range(slots.shape[0]):
+        out_ref[:, r * 128 : (r + 1) * 128] = out[r : r + 1, :]
 
 
 def streamed(tokens_ref, weight_ref, held_ref, rows_ref, sems):
@@ -95,14 +96,14 @@
 
 
 def after(x, *others):
-    anywhere = pl.BlockSpec(memory_space=pl.ANY)
+    whole = pl.BlockSpec(memory_space=pltpu.VMEM)
     return pl.pallas_call(
         lambda *refs: None,
         out_shape=jax.ShapeDtypeStruct(x.shape, x.dtype),
-        in_specs=[anywhere] * (1 + len(others)),
-        out_specs=anywhere,
+        in_specs=[whole] * (1 + len(others)),
+        out_specs=whole,
         input_output_aliases={0: 0},
-        compiler_params=pltpu.CompilerParams(vmem_limit_bytes=1024 * 1024),
+        compiler_params=VMEM,
     )(x, *others)
 
 
@@ -113,12 +114,13 @@
     seq_count = lax.axis_size(SEQ)
     me = lax.axis_index(SEQ)
     core = lax.axis_index("core")
-    side = lax.axis_index("x") % 2
+    side = (lax.axis_index("x") + lax.axis_index("z")) % 2
     half = w_out.shape[0] // 2
     columns = w_out.shape[1]
     width = columns // 2
     swap = [(i, i ^ 1) for i in range(seq_count)]
-    pair = [(i, i ^ 1) for i in range(lax.axis_size("x"))]
+    cores, row = lax.axis_size("core"), lax.axis_size("z") * lax.axis_size("core")
+    pair = [(i, (i // row ^ 1) * row + i % row if i % cores == 0 else i ^ cores) for i in range(seq_count)]
 
     anywhere = pl.BlockSpec(memory_space=pl.ANY)
     whole = pl.BlockSpec(memory_space=pltpu.VMEM)
@@ -155,17 +157,17 @@
         compiler_params=VMEM,
     )(head_of, query[0], bias, kv, kv1, kv2, kv3)
 
-    theirs = lax.ppermute(mixed, "x", pair)
+    theirs = lax.ppermute(mixed, SEQ, pair)
     got = lax.all_to_all(send, SEQ, split_axis=0, concat_axis=0, tiled=True)
     capacity = slot_token.shape[1]
     stats = pl.pallas_call(
         slots_kernel,
-        out_shape=jax.ShapeDtypeStruct((capacity // 128, 128), jnp.float32),
+        out_shape=jax.ShapeDtypeStruct((1, capacity), jnp.float32),
         in_specs=[whole, whole],
         out_specs=whole,
         compiler_params=VMEM,
     )(got, slot_token.reshape(capacity // 128, 128))
-    theirs = after(theirs, got)
+    theirs = after(theirs, stats)
     scratch = [
         pltpu.VMEM((columns, width), jnp.bfloat16),
         pltpu.VMEM((tok_rows, columns), jnp.bfloat16),
@@ -180,7 +182,7 @@
         scratch_shapes=scratch,
         compiler_params=STREAM,
     )(theirs, weight)
-    back = lax.ppermute(away, "x", pair)
+    back = lax.ppermute(away, SEQ, pair)
     result = jax.ShapeDtypeStruct((tok_rows, columns), jnp.bfloat16)
     side = side[None].astype(jnp.int32)
     here = pl.pallas_call(
@@ -200,7 +202,7 @@
         input_output_aliases={1: 0},
         compiler_params=VMEM,
     )(side, here, back, residual[0])
-    return (layer_out[None], stats.reshape(1, capacity))
+    return (layer_out[None], stats)
 
 
 def solution(mesh):

time: 82.1 us -> 80.7 us (0.983)
  blocking collectives: 16.6 us -> 0 us
  starting transfers between devices: 20.6 us -> 28 us
  waiting for transfers between devices: 11.2 us -> 17.2 us
  Pallas kernels: 11.9 us -> 12.9 us
    all_to_all x1 -> x0, blocking collectives: 16.6 us -> none  [local(): got = lax.all_to_all(send, SEQ, split_axis=0, concat_axis=0, tiled=True)]
    all_to_all x0 -> x1, waiting for transfers between devices: none -> 8.47 us  [local(): got = lax.all_to_all(send, SEQ, split_axis=0, concat_axis=0, tiled=True)]
    all_to_all x0 -> x1, starting transfers between devices: none -> 7.56 us  [local(): got = lax.all_to_all(send, SEQ, split_axis=0, concat_axis=0, tiled=True)]
    all_gather x1, waiting for transfers between devices: 1.77 us -> 0.01 us  [local(): weight = lax.all_gather(part, ('fsdp', 'core'), axis=0, tiled=True)]
    unnamed x13 -> x12, local copies, waits for them, and re-layouts: 3.13 us -> 3.2 us
  transfers between devices with their start and end apart: 6 -> 7, of which waited for: 4 -> 4; matrix products, arithmetic and copies ran while one was open for 3% -> 4% of each run, Pallas kernels for 10% -> 11%
where the time goes in v3:
time: 80.7 us; the launch traced here: 80.1 us
  starting transfers between devices  28 us (35%)
  waiting for transfers between devices  17.2 us (21%)
  between operations  14.2 us (18%)
  Pallas kernels  12.9 us (16%)
  local copies, waits for them, and re-layouts  5.84 us (7%)
  other arithmetic  1.94 us (2%)
    all_to_all x1, waiting for transfers between devices, local(): got = lax.all_to_all(send, SEQ, split_axis=0, concat_axis=0, tiled=True)  8.47 us
    all_to_all x1, starting transfers between devices, local(): got = lax.all_to_all(send, SEQ, split_axis=0, concat_axis=0, tiled=True)  7.56 us
    ppermute x1, waiting for transfers between devices, local(): lax.ppermute(kv, SEQ, [(i, (i + 2) % seq_count) for i in range(seq_count)])  7.25 us
    ppermute x1, starting transfers between devices, local(): lax.ppermute(kv, SEQ, [(i, (i + (3 if i % 2 else 1)) % seq_count) for i i...  6.65 us
    ppermute x1, starting transfers between devices, local(): lax.ppermute(kv, SEQ, [(i, (i + 2) % seq_count) for i in range(seq_count)])  4.83 us
    pallas_call x1, Pallas kernels, local(): pl.pallas_call(here_kernel, out_shape=result, in_specs=[scalars, anywhere...  4.37 us
    ppermute x1, starting transfers between devices, local(): kv3 = lax.ppermute(kv1, SEQ, swap)  4.34 us
    pallas_call x1, Pallas kernels, local(): pl.pallas_call(away_kernel, out_shape=jax.ShapeDtypeStruct((tok_rows, wid...  3.4 us
  transfers between devices with their start and end apart: 7, of which 4 were waited for; matrix products, arithmetic and copies ran while one was open for 4% of the time, Pallas kernels for 11%

profile of v3, /device:TPU:1, one launch (start us, length us, event | category | flops | bytes accessed | tf_op | source)
XLA Modules:
  0.0 80.1 jit_solution(2196078412492778581)
XLA Ops:
  7.2 0.0 all-gather.2.cloned.1.call-start
  7.2 1.7 %dynamic_slice.20 = bf16[128,1024]{1,0:T(8,128)(2,1)} dynamic-slice(bf16[256,2048]{1,0:T(8,128)(2,1)} %param.12, s32[]{:T(128)S(6)} %select_n.36, s32[]{:T(128)S(6)} %select_n.37), dynamic_slice_sizes={128,1024} | dynamic-slice | bytes 524292 | tf_op jit(solution)/shard_map/dynamic_slice | solution.py:128
  8.9 0.0 all-gather.2.cloned.1.call-update
  9.0 1.0 %pad_maximum_fusion.kv0_ref = bf16[128,1024]{1,0:T(8,128)(2,1)S(1)} fusion(bf16[128,512]{1,0:T(8,128)(2,1)} %bitcast.18, bf16[128,512]{1,0:T(8,128)(2,1)} %bitcast.19), kind=kLoop, calls=%fused_computation | loop fusion | flops 524288 | bytes 524288 | tf_op jit(solution)/shard_map/concatenate | solution.py:131
  9.9 4.8 %collective-permute-start = (bf16[128,1024]{1,0:T(8,128)(2,1)S(1)}, bf16[128,1024]{1,0:T(8,128)(2,1)S(1)}, u32[]{:S(2)}, u32[]{:S(2)}) collective-permute-start(bf16[128,1024]{1,0:T(8,128)(2,1)S(1)} %pad_maximum_fusion.kv0_ref), channel_id=1, source_target_pairs={{0,16},{8,24},{16,32},{24,40},{32,48},{40,56},{48,64},{56,72},{64,... | collective-permute-start | bytes 786440 | tf_op jit(solution)/shard_map/ppermute | solution.py:132
  14.8 6.6 %collective-permute-start.1 = (bf16[128,1024]{1,0:T(8,128)(2,1)S(1)}, bf16[128,1024]{1,0:T(8,128)(2,1)S(1)}, u32[]{:S(2)}, u32[]{:S(2)}) collective-permute-start(bf16[128,1024]{1,0:T(8,128)(2,1)S(1)} %pad_maximum_fusion.kv0_ref), channel_id=1, source_target_pairs={{0,8},{8,32},{16,24},{24,48},{32,40},{40,64},{48,56},{56,80},{64,7... | collective-permute-start | bytes 786440 | tf_op jit(solution)/shard_map/ppermute | solution.py:133
  21.5 0.9 %pad_dynamic-slice_fusion.2 = (s32[128]{0:T(128)S(1)}, s32[128]{0:T(128)S(1)}, s32[128]{0:T(128)S(1)}, s32[128]{0:T(128)S(1)}) fusion(s32[]{:T(128)S(6)} %select_n.32, s32[8192]{0:T(1024)} %bitcast.20, s32[]{:T(128)S(6)} %select_n.33, s32[]{:T(128)S(6)} %select_n.34, s32[]{:T(128)S(6)} %select_n.31), kind=kLoop, calls=%fused_computation.7 | loop fusion | bytes 34832 | tf_op jit(solution)/shard_map/dynamic_slice | solution.py:140
  22.4 7.2 %collective-permute-done.kv1_ref = bf16[128,1024]{1,0:T(8,128)(2,1)S(1)} collective-permute-done((bf16[128,1024]{1,0:T(8,128)(2,1)S(1)}, bf16[128,1024]{1,0:T(8,128)(2,1)S(1)}, u32[]{:S(2)}, u32[]{:S(2)}) %collective-permute-start) | collective-permute-done | bytes 262176 | tf_op jit(solution)/shard_map/ppermute | solution.py:132
  29.7 4.3 %collective-permute-start.2 = (bf16[128,1024]{1,0:T(8,128)(2,1)S(1)}, bf16[128,1024]{1,0:T(8,128)(2,1)S(1)}, u32[]{:S(2)}, u32[]{:S(2)}) collective-permute-start(bf16[128,1024]{1,0:T(8,128)(2,1)S(1)} %collective-permute-done.kv1_ref), channel_id=1, source_target_pairs={{0,8},{8,0},{16,24},{24,16},{32,40},{40,32},{48,56},{56,48},{64,72... | collective-permute-start | bytes 786440 | tf_op jit(solution)/shard_map/ppermute | solution.py:134
  34.0 0.2 fusion.2.bias_ref
  34.2 0.0 collective-permute-done.1.kv2_ref
  34.2 0.9 %collective-permute-done.2.kv3_ref = bf16[128,1024]{1,0:T(8,128)(2,1)S(1)} collective-permute-done((bf16[128,1024]{1,0:T(8,128)(2,1)S(1)}, bf16[128,1024]{1,0:T(8,128)(2,1)S(1)}, u32[]{:S(2)}, u32[]{:S(2)}) %collective-permute-start.2) | collective-permute-done | bytes 262176 | tf_op jit(solution)/shard_map/ppermute | solution.py:134
  35.2 0.0 copy-start.3
  35.2 1.0 %copy-done.3 = bf16[1,128,2048]{2,1,0:T(8,128)(2,1)S(1)} copy-done((bf16[1,128,2048]{2,1,0:T(8,128)(2,1)S(1)}, bf16[1,128,2048]{2,1,0:T(8,128)(2,1)}, u32[]{:S(2)}) %copy-start.3) | copy-done | bytes 524312
  36.2 0.0 copy-start.5
  36.2 0.7 copy-done.5
  36.9 3.2 %shard_map.95 = (bf16[128,2048]{1,0:T(8,128)(2,1)S(1)}, f32[64,128]{1,0:T(8,128)}) custom-call(s32[64]{0:T(128)S(1)} %copy-done.5, bf16[128,2048]{1,0:T(8,128)(2,1)S(1)} %bitcast.14, f32[512,128]{1,0:T(8,128)S(1)} %fusion.2.bias_ref, bf16[128,1024]{1,0:T(8,128)(2,1)S(1)} %pad_maximum_fusion.kv0_ref, bf16[128,1024]{1,0:T(8,128)(2,1)S(1)} %collective-permute-done.kv1_ref, ...), custom_call_target="tpu_custom_call" | custom-call | tf_op jit(solution)/shard_map/pallas_call | solution.py:148
  40.1 0.0 copy-start.2
  40.1 1.9 %collective-permute-start.3 = (bf16[128,2048]{1,0:T(8,128)(2,1)S(1)}, bf16[128,2048]{1,0:T(8,128)(2,1)S(1)}, u32[]{:S(2)}, u32[]{:S(2)}) collective-permute-start(bf16[128,2048]{1,0:T(8,128)(2,1)S(1)} %get-tuple-element.4.tokens_ref), channel_id=1, source_target_pairs={{0,128},{8,24},{16,144},{24,8},{32,160},{40,56},{48,176},{56,40},{... | collective-permute-start | bytes 1572872 | tf_op jit(solution)/shard_map/ppermute | solution.py:160
  42.0 7.6 %all-to-all-start = ((f32[64,1,128]{2,1,0:T(1,128)}), f32[64,1,128]{2,1,0:T(1,128)S(1)}, u32[]{:S(2)}, u32[]{:S(2)}) async-start(f32[64,1,128]{2,1,0:T(1,128)} %bitcast.7), calls=%async_computation | async-start | bytes 65536 | tf_op jit(solution)/shard_map/all_to_all | solution.py:161
  49.6 0.7 reduce
  50.3 8.5 %all-to-all-done = f32[64,1,128]{2,1,0:T(1,128)S(1)} async-done(((f32[64,1,128]{2,1,0:T(1,128)}), f32[64,1,128]{2,1,0:T(1,128)S(1)}, u32[]{:S(2)}, u32[]{:S(2)}) %all-to-all-start) | async-done | bytes 32800 | tf_op jit(solution)/shard_map/all_to_all | solution.py:161
  58.8 1.2 %shard_map.97.refs_1_ = f32[1,2560]{1,0:T(1,128)} custom-call(f32[64,128]{1,0:T(8,128)S(1)} %bitcast.15, s32[20,128]{1,0:T(8,128)S(1)} %bitcast.16), custom_call_target="tpu_custom_call" | custom-call | tf_op jit(solution)/shard_map/pallas_call | solution.py:163
  60.0 0.0 collective-permute-done.3.refs_0_
  60.0 0.0 copy-start.4
  60.0 0.7 copy-done.4
  60.7 0.0 copy-start
  60.7 0.8 copy-done
  61.5 0.0 copy-start.1
  61.5 0.0 all-gather.2.cloned.1.call-done.weight_ref
  61.5 3.4 %shard_map.99 = bf16[128,1024]{1,0:T(8,128)(2,1)} custom-call(bf16[128,2048]{1,0:T(8,128)(2,1)} %copy-done, bf16[2048,1024]{1,0:T(8,128)(2,1)} %all-gather.2.cloned.1.call-done.weight_ref), custom_call_target="tpu_custom_call" | custom-call | tf_op jit(solution)/shard_map/pallas_call | solution.py:177
  64.9 2.6 %collective-permute-start.4 = (bf16[128,1024]{1,0:T(8,128)(2,1)}, bf16[128,1024]{1,0:T(8,128)(2,1)S(1)}, u32[]{:S(2)}, u32[]{:S(2)}) collective-permute-start(bf16[128,1024]{1,0:T(8,128)(2,1)} %shard_map.99), channel_id=1, source_target_pairs={{0,128},{8,24},{16,144},{24,8},{32,160},{40,56},{48,176},{56,40},{... | collective-permute-start | bytes 786440 | tf_op jit(solution)/shard_map/ppermute | solution.py:185
  67.5 0.0 copy-done.2
  67.5 4.4 %shard_map.96.here_ref = bf16[128,2048]{1,0:T(8,128)(2,1)} custom-call(s32[1]{0:T(128)} %bitcast.side_ref, bf16[128,2048]{1,0:T(8,128)(2,1)} %copy-done.2, bf16[2048,1024]{1,0:T(8,128)(2,1)} %all-gather.2.cloned.1.call-done.weight_ref, bf16[128,2048]{1,0:T(8,128)(2,1)} %bitcast.12), custom_call_target="tpu_custom_call" | custom-call | tf_op jit(solution)/shard_map/pallas_call | solution.py:188
  71.9 0.6 collective-permute-done.4.back_ref
  72.5 0.0 copy-done.1
  72.5 0.8 shard_map.100
  (3 shorter events, 0.0 us)
Async XLA Ops:
  7.2 54.3 %all-gather.2.cloned.1.call-start = ((), (), s32[]{:S(2)}) async-start(), calls=%async_computation.1 | async-start | bytes 4456448 | tf_op jit(solution)/shard_map/all_gather | solution.py:129
  9.9 19.7 %collective-permute-start = (bf16[128,1024]{1,0:T(8,128)(2,1)S(1)}, bf16[128,1024]{1,0:T(8,128)(2,1)S(1)}, u32[]{:S(2)}, u32[]{:S(2)}) collective-permute-start(bf16[128,1024]{1,0:T(8,128)(2,1)S(1)} %pad_maximum_fusion.kv0_ref), channel_id=1, source_target_pairs={{0,16},{8,24},{16,32},{24,40},{32,48},{40,56},{48,64},{56,72},{64,... | collective-permute-start | bytes 786440 | tf_op jit(solution)/shard_map/ppermute | solution.py:132
  14.8 19.5 %collective-permute-start.1 = (bf16[128,1024]{1,0:T(8,128)(2,1)S(1)}, bf16[128,1024]{1,0:T(8,128)(2,1)S(1)}, u32[]{:S(2)}, u32[]{:S(2)}) collective-permute-start(bf16[128,1024]{1,0:T(8,128)(2,1)S(1)} %pad_maximum_fusion.kv0_ref), channel_id=1, source_target_pairs={{0,8},{8,32},{16,24},{24,48},{32,40},{40,64},{48,56},{56,80},{64,7... | collective-permute-start | bytes 786440 | tf_op jit(solution)/shard_map/ppermute | solution.py:133
  29.7 5.5 %collective-permute-start.2 = (bf16[128,1024]{1,0:T(8,128)(2,1)S(1)}, bf16[128,1024]{1,0:T(8,128)(2,1)S(1)}, u32[]{:S(2)}, u32[]{:S(2)}) collective-permute-start(bf16[128,1024]{1,0:T(8,128)(2,1)S(1)} %collective-permute-done.kv1_ref), channel_id=1, source_target_pairs={{0,8},{8,0},{16,24},{24,16},{32,40},{40,32},{48,56},{56,48},{64,72... | collective-permute-start | bytes 786440 | tf_op jit(solution)/shard_map/ppermute | solution.py:134
  35.2 1.0 %copy-start.3 = (bf16[1,128,2048]{2,1,0:T(8,128)(2,1)S(1)}, bf16[1,128,2048]{2,1,0:T(8,128)(2,1)}, u32[]{:S(2)}) copy-start(bf16[1,128,2048]{2,1,0:T(8,128)(2,1)} %param.8) | copy-start | bytes 1572868
  36.2 0.7 copy-start.5
  40.1 27.4 %copy-start.2 = (bf16[128,2048]{1,0:T(8,128)(2,1)}, bf16[128,2048]{1,0:T(8,128)(2,1)S(1)}, u32[]{:S(2)}) copy-start(bf16[128,2048]{1,0:T(8,128)(2,1)S(1)} %get-tuple-element.4.tokens_ref) | copy-start | bytes 1572868
  40.1 19.9 %collective-permute-start.3 = (bf16[128,2048]{1,0:T(8,128)(2,1)S(1)}, bf16[128,2048]{1,0:T(8,128)(2,1)S(1)}, u32[]{:S(2)}, u32[]{:S(2)}) collective-permute-start(bf16[128,2048]{1,0:T(8,128)(2,1)S(1)} %get-tuple-element.4.tokens_ref), channel_id=1, source_target_pairs={{0,128},{8,24},{16,144},{24,8},{32,160},{40,56},{48,176},{56,40},{... | collective-permute-start | bytes 1572872 | tf_op jit(solution)/shard_map/ppermute | solution.py:160
  42.0 16.8 %all-to-all-start = ((f32[64,1,128]{2,1,0:T(1,128)}), f32[64,1,128]{2,1,0:T(1,128)S(1)}, u32[]{:S(2)}, u32[]{:S(2)}) async-start(f32[64,1,128]{2,1,0:T(1,128)} %bitcast.7), calls=%async_computation | async-start | bytes 65536 | tf_op jit(solution)/shard_map/all_to_all | solution.py:161
  60.0 0.7 copy-start.4
  60.7 0.8 copy-start
  61.5 11.0 %copy-start.1 = (bf16[1,128,2048]{2,1,0:T(8,128)(2,1)S(1)}, bf16[1,128,2048]{2,1,0:T(8,128)(2,1)}, u32[]{:S(2)}) copy-start(bf16[1,128,2048]{2,1,0:T(8,128)(2,1)} %param.11) | copy-start | bytes 1572868
  64.9 7.6 %collective-permute-start.4 = (bf16[128,1024]{1,0:T(8,128)(2,1)}, bf16[128,1024]{1,0:T(8,128)(2,1)S(1)}, u32[]{:S(2)}, u32[]{:S(2)}) collective-permute-start(bf16[128,1024]{1,0:T(8,128)(2,1)} %shard_map.99), channel_id=1, source_target_pairs={{0,128},{8,24},{16,144},{24,8},{32,160},{40,56},{48,176},{56,40},{... | collective-permute-start | bytes 786440 | tf_op jit(solution)/shard_map/ppermute | solution.py:185
Sparse Core Ops, SparseCore 0:
  10.1 50.7 all-gather.1

commit v4 on v3

--- a/solution.py
+++ b/solution.py
@@ -95,6 +95,12 @@
     copy.wait()
 
 
+def fetch_kernel(source_ref, out_ref, sem):
+    copy = pltpu.make_async_copy(source_ref, out_ref, sem)
+    copy.start()
+    copy.wait()
+
+
 def after(x, *others):
     whole = pl.BlockSpec(memory_space=pltpu.VMEM)
     return pl.pallas_call(
@@ -131,6 +137,15 @@
     kv = jnp.concatenate([key_proj[0], value_projection_side[0]], axis=1)
     kv1 = lax.ppermute(kv, SEQ, [(i, (i + 2) % seq_count) for i in range(seq_count)])
     kv2 = lax.ppermute(kv, SEQ, [(i, (i + (3 if i % 2 else 1)) % seq_count) for i in range(seq_count)])
+    queries = pl.pallas_call(
+        fetch_kernel,
+        out_shape=jax.ShapeDtypeStruct(query.shape[1:], query.dtype),
+        in_specs=[pl.BlockSpec(memory_space=pl.ANY)],
+        out_specs=pl.BlockSpec(memory_space=pltpu.VMEM),
+        scratch_shapes=[pltpu.SemaphoreType.DMA],
+        compiler_params=VMEM,
+    )(query[0])
+    kv1 = after(kv1, queries)
     kv3 = lax.ppermute(kv1, SEQ, swap)
 
     back_rows = BACK * tok_rows
@@ -155,7 +170,7 @@
         out_specs=(whole, whole),
         scratch_shapes=[pltpu.VMEM((heads, tok_rows), jnp.float32)],
         compiler_params=VMEM,
-    )(head_of, query[0], bias, kv, kv1, kv2, kv3)
+    )(head_of, queries, bias, kv, kv1, kv2, kv3)
 
     theirs = lax.ppermute(mixed, SEQ, pair)
     got = lax.all_to_all(send, SEQ, split_axis=0, concat_axis=0, tiled=True)

time: 80.7 us -> 80.1 us (level)
    ppermute x1, waiting for transfers between devices: 7.25 us -> 6.14 us  [local(): lax.ppermute(kv, SEQ, [(i, (i + 2) % seq_count) for i in range(seq_count)])]
    unnamed x12 -> x14, local copies, waits for them, and re-layouts: 3.2 us -> 3.2 us
  transfers between devices with their start and end apart: 7 -> 7, of which waited for: 4 -> 4; matrix products, arithmetic and copies ran while one was open for 4% -> 3% of each run, Pallas kernels for 11% -> 11%
where the time goes in v4:
time: 80.1 us; the launch traced here: 79.6 us
  starting transfers between devices  28.6 us (36%)
  waiting for transfers between devices  16.7 us (21%)
  between operations  14.2 us (18%)
  Pallas kernels  12.9 us (16%)
  local copies, waits for them, and re-layouts  5.83 us (7%)
  other arithmetic  1.24 us (2%)
    all_to_all x1, waiting for transfers between devices, local(): got = lax.all_to_all(send, SEQ, split_axis=0, concat_axis=0, tiled=True)  9.16 us
    all_to_all x1, starting transfers between devices, local(): got = lax.all_to_all(send, SEQ, split_axis=0, concat_axis=0, tiled=True)  7.56 us
    ppermute x1, starting transfers between devices, local(): lax.ppermute(kv, SEQ, [(i, (i + (3 if i % 2 else 1)) % seq_count) for i i...  6.65 us
    ppermute x1, waiting for transfers between devices, local(): lax.ppermute(kv, SEQ, [(i, (i + 2) % seq_count) for i in range(seq_count)])  6.14 us
    ppermute x1, starting transfers between devices, local(): lax.ppermute(kv, SEQ, [(i, (i + 2) % seq_count) for i in range(seq_count)])  4.83 us
    pallas_call x1, Pallas kernels, local(): pl.pallas_call(here_kernel, out_shape=result, in_specs=[scalars, anywhere...  4.37 us
    ppermute x1, starting transfers between devices, local(): kv3 = lax.ppermute(kv1, SEQ, swap)  4.34 us
    pallas_call x1, Pallas kernels, local(): pl.pallas_call(away_kernel, out_shape=jax.ShapeDtypeStruct((tok_rows, wid...  3.33 us
  transfers between devices with their start and end apart: 7, of which 4 were waited for; matrix products, arithmetic and copies ran while one was open for 3% of the time, Pallas kernels for 11%

profile of v4, /device:TPU:1, one launch (start us, length us, event | category | flops | bytes accessed | tf_op | source)
XLA Modules:
  0.0 79.6 jit_solution(634490042956420080)
XLA Ops:
  7.2 0.0 copy-start.6
  7.2 0.0 all-gather.2.cloned.1.call-start
  7.2 1.7 %dynamic_slice.20 = bf16[128,1024]{1,0:T(8,128)(2,1)} dynamic-slice(bf16[256,2048]{1,0:T(8,128)(2,1)} %param.12, s32[]{:T(128)S(6)} %select_n.36, s32[]{:T(128)S(6)} %select_n.37), dynamic_slice_sizes={128,1024} | dynamic-slice | bytes 524292 | tf_op jit(solution)/shard_map/dynamic_slice | solution.py:134
  8.9 0.0 all-gather.2.cloned.1.call-update
  8.9 1.0 %pad_maximum_fusion.kv0_ref = bf16[128,1024]{1,0:T(8,128)(2,1)S(1)} fusion(bf16[128,512]{1,0:T(8,128)(2,1)} %bitcast.18, bf16[128,512]{1,0:T(8,128)(2,1)} %bitcast.19), kind=kLoop, calls=%fused_computation | loop fusion | flops 524288 | bytes 524288 | tf_op jit(solution)/shard_map/concatenate | solution.py:137
  9.9 4.8 %collective-permute-start = (bf16[128,1024]{1,0:T(8,128)(2,1)S(1)}, bf16[128,1024]{1,0:T(8,128)(2,1)S(1)}, u32[]{:S(2)}, u32[]{:S(2)}) collective-permute-start(bf16[128,1024]{1,0:T(8,128)(2,1)S(1)} %pad_maximum_fusion.kv0_ref), channel_id=1, source_target_pairs={{0,16},{8,24},{16,32},{24,40},{32,48},{40,56},{48,64},{56,72},{64,... | collective-permute-start | bytes 786440 | tf_op jit(solution)/shard_map/ppermute | solution.py:138
  14.8 6.6 %collective-permute-start.1 = (bf16[128,1024]{1,0:T(8,128)(2,1)S(1)}, bf16[128,1024]{1,0:T(8,128)(2,1)S(1)}, u32[]{:S(2)}, u32[]{:S(2)}) collective-permute-start(bf16[128,1024]{1,0:T(8,128)(2,1)S(1)} %pad_maximum_fusion.kv0_ref), channel_id=1, source_target_pairs={{0,8},{8,32},{16,24},{24,48},{32,40},{40,64},{48,56},{56,80},{64,7... | collective-permute-start | bytes 786440 | tf_op jit(solution)/shard_map/ppermute | solution.py:139
  21.5 0.0 copy-start.3
  21.5 1.0 %copy-done.3 = bf16[1,128,2048]{2,1,0:T(8,128)(2,1)S(1)} copy-done((bf16[1,128,2048]{2,1,0:T(8,128)(2,1)S(1)}, bf16[1,128,2048]{2,1,0:T(8,128)(2,1)}, u32[]{:S(2)}) %copy-start.3) | copy-done | bytes 524312
  22.6 0.9 %pad_dynamic-slice_fusion.2 = (s32[128]{0:T(128)S(1)}, s32[128]{0:T(128)S(1)}, s32[128]{0:T(128)S(1)}, s32[128]{0:T(128)S(1)}) fusion(s32[]{:T(128)S(6)} %select_n.32, s32[8192]{0:T(1024)} %bitcast.20, s32[]{:T(128)S(6)} %select_n.33, s32[]{:T(128)S(6)} %select_n.34, s32[]{:T(128)S(6)} %select_n.31), kind=kLoop, calls=%fused_computation.7 | loop fusion | bytes 34832 | tf_op jit(solution)/shard_map/dynamic_slice | solution.py:155
  23.5 6.1 %collective-permute-done.refs_0_ = bf16[128,1024]{1,0:T(8,128)(2,1)S(1)} collective-permute-done((bf16[128,1024]{1,0:T(8,128)(2,1)S(1)}, bf16[128,1024]{1,0:T(8,128)(2,1)S(1)}, u32[]{:S(2)}, u32[]{:S(2)}) %collective-permute-start) | collective-permute-done | bytes 262176 | tf_op jit(solution)/shard_map/ppermute | solution.py:138
  29.7 4.3 %collective-permute-start.2 = (bf16[128,1024]{1,0:T(8,128)(2,1)S(1)}, bf16[128,1024]{1,0:T(8,128)(2,1)S(1)}, u32[]{:S(2)}, u32[]{:S(2)}) collective-permute-start(bf16[128,1024]{1,0:T(8,128)(2,1)S(1)} %shard_map.96.kv1_ref), channel_id=1, source_target_pairs={{0,8},{8,0},{16,24},{24,16},{32,40},{40,32},{48,56},{56,48},{64,72... | collective-permute-start | bytes 786440 | tf_op jit(solution)/shard_map/ppermute | solution.py:149
  34.0 0.2 fusion.2.bias_ref
  34.2 0.0 collective-permute-done.1.kv2_ref
  34.2 0.9 %collective-permute-done.2.kv3_ref = bf16[128,1024]{1,0:T(8,128)(2,1)S(1)} collective-permute-done((bf16[128,1024]{1,0:T(8,128)(2,1)S(1)}, bf16[128,1024]{1,0:T(8,128)(2,1)S(1)}, u32[]{:S(2)}, u32[]{:S(2)}) %collective-permute-start.2) | collective-permute-done | bytes 262176 | tf_op jit(solution)/shard_map/ppermute | solution.py:149
  35.2 0.0 copy-start.5
  35.2 0.7 copy-done.5
  35.8 3.2 %shard_map.97 = (bf16[128,2048]{1,0:T(8,128)(2,1)S(1)}, f32[64,128]{1,0:T(8,128)}) custom-call(s32[64]{0:T(128)S(1)} %copy-done.5, bf16[128,2048]{1,0:T(8,128)(2,1)S(1)} %shard_map.95.refs_1_.q_ref, f32[512,128]{1,0:T(8,128)S(1)} %fusion.2.bias_ref, bf16[128,1024]{1,0:T(8,128)(2,1)S(1)} %pad_maximum_fusion.kv0_ref, bf16[128,1024]{1,0:T(8,128)(2,1)S(1)} %shard_map.96.kv1_ref, ...), custom_call_target="tpu_custom_call" | custom-call | tf_op jit(solution)/shard_map/pallas_call | solution.py:163
  39.0 0.0 copy-start.2
  39.1 1.9 %collective-permute-start.3 = (bf16[128,2048]{1,0:T(8,128)(2,1)S(1)}, bf16[128,2048]{1,0:T(8,128)(2,1)S(1)}, u32[]{:S(2)}, u32[]{:S(2)}) collective-permute-start(bf16[128,2048]{1,0:T(8,128)(2,1)S(1)} %get-tuple-element.4.tokens_ref), channel_id=1, source_target_pairs={{0,128},{8,24},{16,144},{24,8},{32,160},{40,56},{48,176},{56,40},{... | collective-permute-start | bytes 1572872 | tf_op jit(solution)/shard_map/ppermute | solution.py:175
  41.0 7.6 %all-to-all-start = ((f32[64,1,128]{2,1,0:T(1,128)}), f32[64,1,128]{2,1,0:T(1,128)S(1)}, u32[]{:S(2)}, u32[]{:S(2)}) async-start(f32[64,1,128]{2,1,0:T(1,128)} %bitcast.7), calls=%async_computation | async-start | bytes 65536 | tf_op jit(solution)/shard_map/all_to_all | solution.py:176
  48.5 0.0 copy-done.6
  48.6 9.2 %all-to-all-done = f32[64,1,128]{2,1,0:T(1,128)S(1)} async-done(((f32[64,1,128]{2,1,0:T(1,128)}), f32[64,1,128]{2,1,0:T(1,128)S(1)}, u32[]{:S(2)}, u32[]{:S(2)}) %all-to-all-start) | async-done | bytes 32800 | tf_op jit(solution)/shard_map/all_to_all | solution.py:176
  57.8 1.2 %shard_map.99.refs_1_ = f32[1,2560]{1,0:T(1,128)} custom-call(f32[64,128]{1,0:T(8,128)S(1)} %bitcast.15, s32[20,128]{1,0:T(8,128)S(1)} %bitcast.16), custom_call_target="tpu_custom_call" | custom-call | tf_op jit(solution)/shard_map/pallas_call | solution.py:178
  58.9 0.0 collective-permute-done.3.refs_0_
  58.9 0.0 copy-start.4
  58.9 0.7 copy-done.4
  59.6 0.0 copy-start
  59.6 0.8 copy-done
  60.4 0.0 copy-start.1
  60.4 0.5 all-gather.2.cloned.1.call-done.weight_ref
  60.9 3.3 %shard_map.101 = bf16[128,1024]{1,0:T(8,128)(2,1)} custom-call(bf16[128,2048]{1,0:T(8,128)(2,1)} %copy-done, bf16[2048,1024]{1,0:T(8,128)(2,1)} %all-gather.2.cloned.1.call-done.weight_ref), custom_call_target="tpu_custom_call" | custom-call | tf_op jit(solution)/shard_map/pallas_call | solution.py:192
  64.2 3.3 %collective-permute-start.4 = (bf16[128,1024]{1,0:T(8,128)(2,1)}, bf16[128,1024]{1,0:T(8,128)(2,1)S(1)}, u32[]{:S(2)}, u32[]{:S(2)}) collective-permute-start(bf16[128,1024]{1,0:T(8,128)(2,1)} %shard_map.101), channel_id=1, source_target_pairs={{0,128},{8,24},{16,144},{24,8},{32,160},{40,56},{48,176},{56,40},{... | collective-permute-start | bytes 786440 | tf_op jit(solution)/shard_map/ppermute | solution.py:200
  67.5 0.0 copy-done.2
  67.5 4.4 %shard_map.98.here_ref = bf16[128,2048]{1,0:T(8,128)(2,1)} custom-call(s32[1]{0:T(128)} %bitcast.side_ref, bf16[128,2048]{1,0:T(8,128)(2,1)} %copy-done.2, bf16[2048,1024]{1,0:T(8,128)(2,1)} %all-gather.2.cloned.1.call-done.weight_ref, bf16[128,2048]{1,0:T(8,128)(2,1)} %bitcast.12), custom_call_target="tpu_custom_call" | custom-call | tf_op jit(solution)/shard_map/pallas_call | solution.py:203
  71.9 0.0 collective-permute-done.4.back_ref
  71.9 0.0 copy-done.1
  71.9 0.8 shard_map.102
  (6 shorter events, 0.1 us)
Async XLA Ops:
  7.2 41.4 %copy-start.6 = (s32[1,2560]{1,0:T(1,128)S(1)}, s32[1,2560]{1,0:T(1,128)}, u32[]{:S(2)}) copy-start(s32[1,2560]{1,0:T(1,128)} %param.14) | copy-start | bytes 30724
  7.2 53.7 %all-gather.2.cloned.1.call-start = ((), (), s32[]{:S(2)}) async-start(), calls=%async_computation.1 | async-start | bytes 4456448 | tf_op jit(solution)/shard_map/all_gather | solution.py:135
  9.9 19.7 %collective-permute-start = (bf16[128,1024]{1,0:T(8,128)(2,1)S(1)}, bf16[128,1024]{1,0:T(8,128)(2,1)S(1)}, u32[]{:S(2)}, u32[]{:S(2)}) collective-permute-start(bf16[128,1024]{1,0:T(8,128)(2,1)S(1)} %pad_maximum_fusion.kv0_ref), channel_id=1, source_target_pairs={{0,16},{8,24},{16,32},{24,40},{32,48},{40,56},{48,64},{56,72},{64,... | collective-permute-start | bytes 786440 | tf_op jit(solution)/shard_map/ppermute | solution.py:138
  14.8 19.5 %collective-permute-start.1 = (bf16[128,1024]{1,0:T(8,128)(2,1)S(1)}, bf16[128,1024]{1,0:T(8,128)(2,1)S(1)}, u32[]{:S(2)}, u32[]{:S(2)}) collective-permute-start(bf16[128,1024]{1,0:T(8,128)(2,1)S(1)} %pad_maximum_fusion.kv0_ref), channel_id=1, source_target_pairs={{0,8},{8,32},{16,24},{24,48},{32,40},{40,64},{48,56},{56,80},{64,7... | collective-permute-start | bytes 786440 | tf_op jit(solution)/shard_map/ppermute | solution.py:139
  21.5 1.0 %copy-start.3 = (bf16[1,128,2048]{2,1,0:T(8,128)(2,1)S(1)}, bf16[1,128,2048]{2,1,0:T(8,128)(2,1)}, u32[]{:S(2)}) copy-start(bf16[1,128,2048]{2,1,0:T(8,128)(2,1)} %param.8) | copy-start | bytes 1572868
  29.7 5.5 %collective-permute-start.2 = (bf16[128,1024]{1,0:T(8,128)(2,1)S(1)}, bf16[128,1024]{1,0:T(8,128)(2,1)S(1)}, u32[]{:S(2)}, u32[]{:S(2)}) collective-permute-start(bf16[128,1024]{1,0:T(8,128)(2,1)S(1)} %shard_map.96.kv1_ref), channel_id=1, source_target_pairs={{0,8},{8,0},{16,24},{24,16},{32,40},{40,32},{48,56},{56,48},{64,72... | collective-permute-start | bytes 786440 | tf_op jit(solution)/shard_map/ppermute | solution.py:149
  35.2 0.7 copy-start.5
  39.0 28.5 %copy-start.2 = (bf16[128,2048]{1,0:T(8,128)(2,1)}, bf16[128,2048]{1,0:T(8,128)(2,1)S(1)}, u32[]{:S(2)}) copy-start(bf16[128,2048]{1,0:T(8,128)(2,1)S(1)} %get-tuple-element.4.tokens_ref) | copy-start | bytes 1572868
  39.1 19.9 %collective-permute-start.3 = (bf16[128,2048]{1,0:T(8,128)(2,1)S(1)}, bf16[128,2048]{1,0:T(8,128)(2,1)S(1)}, u32[]{:S(2)}, u32[]{:S(2)}) collective-permute-start(bf16[128,2048]{1,0:T(8,128)(2,1)S(1)} %get-tuple-element.4.tokens_ref), channel_id=1, source_target_pairs={{0,128},{8,24},{16,144},{24,8},{32,160},{40,56},{48,176},{56,40},{... | collective-permute-start | bytes 1572872 | tf_op jit(solution)/shard_map/ppermute | solution.py:175
  41.0 16.8 %all-to-all-start = ((f32[64,1,128]{2,1,0:T(1,128)}), f32[64,1,128]{2,1,0:T(1,128)S(1)}, u32[]{:S(2)}, u32[]{:S(2)}) async-start(f32[64,1,128]{2,1,0:T(1,128)} %bitcast.7), calls=%async_computation | async-start | bytes 65536 | tf_op jit(solution)/shard_map/all_to_all | solution.py:176
  58.9 0.7 copy-start.4
  59.6 0.8 copy-start
  60.4 11.5 %copy-start.1 = (bf16[1,128,2048]{2,1,0:T(8,128)(2,1)S(1)}, bf16[1,128,2048]{2,1,0:T(8,128)(2,1)}, u32[]{:S(2)}) copy-start(bf16[1,128,2048]{2,1,0:T(8,128)(2,1)} %param.11) | copy-start | bytes 1572868
  64.2 7.7 %collective-permute-start.4 = (bf16[128,1024]{1,0:T(8,128)(2,1)}, bf16[128,1024]{1,0:T(8,128)(2,1)S(1)}, u32[]{:S(2)}, u32[]{:S(2)}) collective-permute-start(bf16[128,1024]{1,0:T(8,128)(2,1)} %shard_map.101), channel_id=1, source_target_pairs={{0,128},{8,24},{16,144},{24,8},{32,160},{40,56},{48,176},{56,40},{... | collective-permute-start | bytes 786440 | tf_op jit(solution)/shard_map/ppermute | solution.py:200
Sparse Core Ops, SparseCore 0:
  10.1 50.7 all-gather.1

commit v5 on v4

--- a/solution.py
+++ b/solution.py
@@ -14,7 +14,6 @@
 SCALE = 1.0 / math.sqrt(HEAD_SIZE)
 SEQ = ("x", "z", "core")
 VMEM = pltpu.CompilerParams(vmem_limit_bytes=14 * 1024 * 1024)
-STREAM = pltpu.CompilerParams(vmem_limit_bytes=56 * 1024 * 1024)
 
 
 def attend_kernel(heads, kv_heads, head_of_ref, q_ref, bias_ref, kv0_ref, kv1_ref, kv2_ref, kv3_ref, mixed_ref, send_ref, lt_ref):
@@ -53,32 +52,15 @@
         out_ref[:, r * 128 : (r + 1) * 128] = out[r : r + 1, :]
 
 
-def streamed(tokens_ref, weight_ref, held_ref, rows_ref, sems):
-    count = sems.shape[0] - 1
-    step = weight_ref.shape[0] // count
-    parts = [pl.ds(i * step, step) for i in range(count)]
-    tokens = pltpu.make_async_copy(tokens_ref, rows_ref, sems.at[count])
-    copies = [pltpu.make_async_copy(weight_ref.at[p], held_ref.at[p], sems.at[i]) for i, p in enumerate(parts)]
-    tokens.start()
-    for copy in copies:
-        copy.start()
-    tokens.wait()
-    total = None
-    for copy, part in zip(copies, parts):
-        copy.wait()
-        product = jnp.dot(rows_ref[:, part], held_ref[part, :], preferred_element_type=jnp.float32)
-        total = product if total is None else total + product
-    return total
-
-
-def away_kernel(tokens_ref, weight_ref, out_ref, held_ref, rows_ref, sems):
-    out_ref[...] = streamed(tokens_ref, weight_ref, held_ref, rows_ref, sems).astype(jnp.bfloat16)
-
-
-def here_kernel(side_ref, tokens_ref, weight_ref, residual_ref, out_ref, held_ref, rows_ref, sems, half_ref, sem):
+def away_kernel(tokens_ref, weight_ref, out_ref):
+    total = jnp.dot(tokens_ref[...], weight_ref[...], preferred_element_type=jnp.float32)
+    out_ref[...] = total.astype(jnp.bfloat16)
+
+
+def here_kernel(side_ref, tokens_ref, weight_ref, residual_ref, out_ref, half_ref, sem):
     width = half_ref.shape[1]
     mine = pl.ds(pl.multiple_of(side_ref[0] * width, width), width)
-    total = streamed(tokens_ref, weight_ref, held_ref, rows_ref, sems)
+    total = jnp.dot(tokens_ref[...], weight_ref[...], preferred_element_type=jnp.float32)
     half_ref[...] = (residual_ref[:, mine].astype(jnp.float32) + total).astype(jnp.bfloat16)
     copy = pltpu.make_async_copy(half_ref, out_ref.at[:, mine], sem)
     copy.start()
@@ -183,19 +165,13 @@
         compiler_params=VMEM,
     )(got, slot_token.reshape(capacity // 128, 128))
     theirs = after(theirs, stats)
-    scratch = [
-        pltpu.VMEM((columns, width), jnp.bfloat16),
-        pltpu.VMEM((tok_rows, columns), jnp.bfloat16),
-        pltpu.SemaphoreType.DMA((9,)),
-    ]
     half_scratch = [pltpu.VMEM((tok_rows, width), jnp.bfloat16), pltpu.SemaphoreType.DMA]
     away = pl.pallas_call(
         away_kernel,
         out_shape=jax.ShapeDtypeStruct((tok_rows, width), jnp.bfloat16),
-        in_specs=[anywhere, anywhere],
+        in_specs=[whole, whole],
         out_specs=whole,
-        scratch_shapes=scratch,
-        compiler_params=STREAM,
+        compiler_params=VMEM,
     )(theirs, weight)
     back = lax.ppermute(away, SEQ, pair)
     result = jax.ShapeDtypeStruct((tok_rows, columns), jnp.bfloat16)
@@ -203,10 +179,10 @@
     here = pl.pallas_call(
         here_kernel,
         out_shape=result,
-        in_specs=[scalars, anywhere, anywhere, whole],
+        in_specs=[scalars] + [whole] * 3,
         out_specs=anywhere,
-        scratch_shapes=scratch + half_scratch,
-        compiler_params=STREAM,
+        scratch_shapes=half_scratch,
+        compiler_params=VMEM,
     )(side, mixed, weight, residual[0])
     layer_out = pl.pallas_call(
         join_kernel,

time: 80.1 us -> 80 us (level)
  Pallas kernels: 12.9 us -> 7.41 us
  waiting for transfers between devices: 16.7 us -> 20.7 us
  local copies, waits for them, and re-layouts: 5.83 us -> 7.22 us
    pallas_call x1, Pallas kernels: 4.37 us -> 1.49 us  [local(): pl.pallas_call(here_kernel, out_shape=result, in_specs=[scalars] + [whole...]
    ppermute x1, waiting for transfers between devices: 0.01 us -> 2.61 us  [local(): back = lax.ppermute(away, SEQ, pair)]
    pallas_call x1, Pallas kernels: 3.33 us -> 0.72 us  [local(): pl.pallas_call(away_kernel, out_shape=jax.ShapeDtypeStruct((tok_rows, wid...]
    unnamed x14, local copies, waits for them, and re-layouts: 3.2 us -> 4.6 us
    all_gather x1, waiting for transfers between devices: 0.48 us -> 1.79 us  [local(): weight = lax.all_gather(part, ('fsdp', 'core'), axis=0, tiled=True)]
  transfers between devices with their start and end apart: 7 -> 7, of which waited for: 4 -> 5; matrix products, arithmetic and copies ran while one was open for 3% -> 3% of each run, Pallas kernels for 11% -> 7%
where the time goes in v5:
time: 80 us; the launch traced here: 79.6 us
  starting transfers between devices  28.7 us (36%)
  waiting for transfers between devices  20.7 us (26%)
  between operations  14.2 us (18%)
  Pallas kernels  7.41 us (9%)
  local copies, waits for them, and re-layouts  7.22 us (9%)
  other arithmetic  1.24 us (2%)
    all_to_all x1, waiting for transfers between devices, local(): got = lax.all_to_all(send, SEQ, split_axis=0, concat_axis=0, tiled=True)  9.24 us
    all_to_all x1, starting transfers between devices, local(): got = lax.all_to_all(send, SEQ, split_axis=0, concat_axis=0, tiled=True)  7.43 us
    ppermute x1, starting transfers between devices, local(): lax.ppermute(kv, SEQ, [(i, (i + (3 if i % 2 else 1)) % seq_count) for i i...  6.65 us
    ppermute x1, waiting for transfers between devices, local(): lax.ppermute(kv, SEQ, [(i, (i + 2) % seq_count) for i in range(seq_count)])  6.14 us
    ppermute x1, starting transfers between devices, local(): lax.ppermute(kv, SEQ, [(i, (i + 2) % seq_count) for i in range(seq_count)])  4.83 us
    unnamed x14, local copies, waits for them, and re-layouts  4.6 us
    ppermute x1, starting transfers between devices, local(): kv3 = lax.ppermute(kv1, SEQ, swap)  4.47 us
    ppermute x1, starting transfers between devices, local(): back = lax.ppermute(away, SEQ, pair)  3.41 us
  transfers between devices with their start and end apart: 7, of which 5 were waited for; matrix products, arithmetic and copies ran while one was open for 3% of the time, Pallas kernels for 7%

profile of v5, /device:TPU:1, one launch (start us, length us, event | category | flops | bytes accessed | tf_op | source)
XLA Modules:
  0.0 79.6 jit_solution(6983936446204941307)
XLA Ops:
  7.2 0.0 copy-start.6
  7.2 0.0 all-gather.2.cloned.1.call-start
  7.2 1.7 %dynamic_slice.20 = bf16[128,1024]{1,0:T(8,128)(2,1)} dynamic-slice(bf16[256,2048]{1,0:T(8,128)(2,1)} %param.12, s32[]{:T(128)S(6)} %select_n.36, s32[]{:T(128)S(6)} %select_n.37), dynamic_slice_sizes={128,1024} | dynamic-slice | bytes 524292 | tf_op jit(solution)/shard_map/dynamic_slice | solution.py:116
  8.9 0.0 all-gather.2.cloned.1.call-update
  8.9 1.0 %pad_maximum_fusion.kv0_ref = bf16[128,1024]{1,0:T(8,128)(2,1)S(1)} fusion(bf16[128,512]{1,0:T(8,128)(2,1)} %bitcast.18, bf16[128,512]{1,0:T(8,128)(2,1)} %bitcast.19), kind=kLoop, calls=%fused_computation | loop fusion | flops 524288 | bytes 524288 | tf_op jit(solution)/shard_map/concatenate | solution.py:119
  9.9 4.8 %collective-permute-start = (bf16[128,1024]{1,0:T(8,128)(2,1)S(1)}, bf16[128,1024]{1,0:T(8,128)(2,1)S(1)}, u32[]{:S(2)}, u32[]{:S(2)}) collective-permute-start(bf16[128,1024]{1,0:T(8,128)(2,1)S(1)} %pad_maximum_fusion.kv0_ref), channel_id=1, source_target_pairs={{0,16},{8,24},{16,32},{24,40},{32,48},{40,56},{48,64},{56,72},{64,... | collective-permute-start | bytes 786440 | tf_op jit(solution)/shard_map/ppermute | solution.py:120
  14.8 6.6 %collective-permute-start.1 = (bf16[128,1024]{1,0:T(8,128)(2,1)S(1)}, bf16[128,1024]{1,0:T(8,128)(2,1)S(1)}, u32[]{:S(2)}, u32[]{:S(2)}) collective-permute-start(bf16[128,1024]{1,0:T(8,128)(2,1)S(1)} %pad_maximum_fusion.kv0_ref), channel_id=1, source_target_pairs={{0,8},{8,32},{16,24},{24,48},{32,40},{40,64},{48,56},{56,80},{64,7... | collective-permute-start | bytes 786440 | tf_op jit(solution)/shard_map/ppermute | solution.py:121
  21.5 0.0 copy-start.3
  21.5 1.0 %copy-done.3 = bf16[1,128,2048]{2,1,0:T(8,128)(2,1)S(1)} copy-done((bf16[1,128,2048]{2,1,0:T(8,128)(2,1)S(1)}, bf16[1,128,2048]{2,1,0:T(8,128)(2,1)}, u32[]{:S(2)}) %copy-start.3) | copy-done | bytes 524312
  22.6 0.9 %pad_dynamic-slice_fusion.2 = (s32[128]{0:T(128)S(1)}, s32[128]{0:T(128)S(1)}, s32[128]{0:T(128)S(1)}, s32[128]{0:T(128)S(1)}) fusion(s32[]{:T(128)S(6)} %select_n.32, s32[8192]{0:T(1024)} %bitcast.20, s32[]{:T(128)S(6)} %select_n.33, s32[]{:T(128)S(6)} %select_n.34, s32[]{:T(128)S(6)} %select_n.31), kind=kLoop, calls=%fused_computation.7 | loop fusion | bytes 34832 | tf_op jit(solution)/shard_map/dynamic_slice | solution.py:137
  23.5 6.1 %collective-permute-done.refs_0_ = bf16[128,1024]{1,0:T(8,128)(2,1)S(1)} collective-permute-done((bf16[128,1024]{1,0:T(8,128)(2,1)S(1)}, bf16[128,1024]{1,0:T(8,128)(2,1)S(1)}, u32[]{:S(2)}, u32[]{:S(2)}) %collective-permute-start) | collective-permute-done | bytes 262176 | tf_op jit(solution)/shard_map/ppermute | solution.py:120
  29.7 0.0 copy-start.2
  29.7 4.5 %collective-permute-start.2 = (bf16[128,1024]{1,0:T(8,128)(2,1)S(1)}, bf16[128,1024]{1,0:T(8,128)(2,1)S(1)}, u32[]{:S(2)}, u32[]{:S(2)}) collective-permute-start(bf16[128,1024]{1,0:T(8,128)(2,1)S(1)} %shard_map.96.kv1_ref), channel_id=1, source_target_pairs={{0,8},{8,0},{16,24},{24,16},{32,40},{40,32},{48,56},{56,48},{64,72... | collective-permute-start | bytes 786440 | tf_op jit(solution)/shard_map/ppermute | solution.py:131
  34.2 0.2 fusion.2.bias_ref
  34.4 0.0 collective-permute-done.1.kv2_ref
  34.4 0.9 %collective-permute-done.2.kv3_ref = bf16[128,1024]{1,0:T(8,128)(2,1)S(1)} collective-permute-done((bf16[128,1024]{1,0:T(8,128)(2,1)S(1)}, bf16[128,1024]{1,0:T(8,128)(2,1)S(1)}, u32[]{:S(2)}, u32[]{:S(2)}) %collective-permute-start.2) | collective-permute-done | bytes 262176 | tf_op jit(solution)/shard_map/ppermute | solution.py:131
  35.3 0.0 copy-start.5
  35.3 0.7 copy-done.5
  35.9 3.2 %shard_map.97 = (bf16[128,2048]{1,0:T(8,128)(2,1)S(1)}, f32[64,128]{1,0:T(8,128)}) custom-call(s32[64]{0:T(128)S(1)} %copy-done.5, bf16[128,2048]{1,0:T(8,128)(2,1)S(1)} %shard_map.95.refs_1_.q_ref, f32[512,128]{1,0:T(8,128)S(1)} %fusion.2.bias_ref, bf16[128,1024]{1,0:T(8,128)(2,1)S(1)} %pad_maximum_fusion.kv0_ref, bf16[128,1024]{1,0:T(8,128)(2,1)S(1)} %shard_map.96.kv1_ref, ...), custom_call_target="tpu_custom_call" | custom-call | tf_op jit(solution)/shard_map/pallas_call | solution.py:145
  39.2 1.9 %collective-permute-start.3 = (bf16[128,2048]{1,0:T(8,128)(2,1)S(1)}, bf16[128,2048]{1,0:T(8,128)(2,1)S(1)}, u32[]{:S(2)}, u32[]{:S(2)}) collective-permute-start(bf16[128,2048]{1,0:T(8,128)(2,1)S(1)} %get-tuple-element.4.tokens_ref), channel_id=1, source_target_pairs={{0,128},{8,24},{16,144},{24,8},{32,160},{40,56},{48,176},{56,40},{... | collective-permute-start | bytes 1572872 | tf_op jit(solution)/shard_map/ppermute | solution.py:157
  41.1 7.4 %all-to-all-start = ((f32[64,1,128]{2,1,0:T(1,128)}), f32[64,1,128]{2,1,0:T(1,128)S(1)}, u32[]{:S(2)}, u32[]{:S(2)}) async-start(f32[64,1,128]{2,1,0:T(1,128)} %bitcast.7), calls=%async_computation | async-start | bytes 65536 | tf_op jit(solution)/shard_map/all_to_all | solution.py:158
  48.5 0.0 copy-done.6
  48.6 9.2 %all-to-all-done = f32[64,1,128]{2,1,0:T(1,128)S(1)} async-done(((f32[64,1,128]{2,1,0:T(1,128)}), f32[64,1,128]{2,1,0:T(1,128)S(1)}, u32[]{:S(2)}, u32[]{:S(2)}) %all-to-all-start) | async-done | bytes 32800 | tf_op jit(solution)/shard_map/all_to_all | solution.py:158
  57.8 1.2 %shard_map.99.refs_1_ = f32[1,2560]{1,0:T(1,128)} custom-call(f32[64,128]{1,0:T(8,128)S(1)} %bitcast.15, s32[20,128]{1,0:T(8,128)S(1)} %bitcast.16), custom_call_target="tpu_custom_call" | custom-call | tf_op jit(solution)/shard_map/pallas_call | solution.py:160
  59.0 0.0 collective-permute-done.3.refs_0_
  59.0 0.0 copy-start.4
  59.0 0.7 copy-done.4
  59.7 1.8 %all-gather.2.cloned.1.call-done.weight_ref = bf16[2048,1024]{1,0:T(8,128)(2,1)} async-done(((bf16[128,1024]{1,0:T(8,128)(2,1)}), bf16[2048,1024]{1,0:T(8,128)(2,1)}) %all-gather.2.cloned.1.call-update) | async-done | bytes 4194320 | tf_op jit(solution)/shard_map/all_gather | solution.py:117
  61.5 0.0 copy-start
  61.5 2.2 %copy-done = bf16[2048,1024]{1,0:T(8,128)(2,1)S(1)} copy-done((bf16[2048,1024]{1,0:T(8,128)(2,1)S(1)}, bf16[2048,1024]{1,0:T(8,128)(2,1)}, u32[]{:S(2)}) %copy-start) | copy-done | bytes 4194328
  63.6 0.0 copy-start.1
  63.7 0.7 shard_map.101
  64.4 3.4 %collective-permute-start.4 = (bf16[128,1024]{1,0:T(8,128)(2,1)S(1)}, bf16[128,1024]{1,0:T(8,128)(2,1)S(1)}, u32[]{:S(2)}, u32[]{:S(2)}) collective-permute-start(bf16[128,1024]{1,0:T(8,128)(2,1)S(1)} %shard_map.101), channel_id=1, source_target_pairs={{0,128},{8,24},{16,144},{24,8},{32,160},{40,56},{48,176},{56,40},{... | collective-permute-start | bytes 786440 | tf_op jit(solution)/shard_map/ppermute | solution.py:176
  67.8 0.0 copy-done.2
  67.8 0.0 copy-done.1
  67.8 1.5 %shard_map.98.here_ref = bf16[128,2048]{1,0:T(8,128)(2,1)} custom-call(s32[1]{0:T(128)} %bitcast.side_ref, bf16[128,2048]{1,0:T(8,128)(2,1)S(1)} %get-tuple-element.4.tokens_ref, bf16[2048,1024]{1,0:T(8,128)(2,1)S(1)} %copy-done.1, bf16[128,2048]{1,0:T(8,128)(2,1)S(1)} %bitcast.12), custom_call_target="tpu_custom_call" | custom-call | tf_op jit(solution)/shard_map/pallas_call | solution.py:179
  69.3 2.6 %collective-permute-done.4.back_ref = bf16[128,1024]{1,0:T(8,128)(2,1)S(1)} collective-permute-done((bf16[128,1024]{1,0:T(8,128)(2,1)S(1)}, bf16[128,1024]{1,0:T(8,128)(2,1)S(1)}, u32[]{:S(2)}, u32[]{:S(2)}) %collective-permute-start.4) | collective-permute-done | bytes 262176 | tf_op jit(solution)/shard_map/ppermute | solution.py:176
  71.9 0.8 shard_map.102
  (6 shorter events, 0.1 us)
Async XLA Ops:
  7.2 41.4 %copy-start.6 = (s32[1,2560]{1,0:T(1,128)S(1)}, s32[1,2560]{1,0:T(1,128)}, u32[]{:S(2)}) copy-start(s32[1,2560]{1,0:T(1,128)} %param.14) | copy-start | bytes 30724
  7.2 54.3 %all-gather.2.cloned.1.call-start = ((), (), s32[]{:S(2)}) async-start(), calls=%async_computation.1 | async-start | bytes 4456448 | tf_op jit(solution)/shard_map/all_gather | solution.py:117
  9.9 19.7 %collective-permute-start = (bf16[128,1024]{1,0:T(8,128)(2,1)S(1)}, bf16[128,1024]{1,0:T(8,128)(2,1)S(1)}, u32[]{:S(2)}, u32[]{:S(2)}) collective-permute-start(bf16[128,1024]{1,0:T(8,128)(2,1)S(1)} %pad_maximum_fusion.kv0_ref), channel_id=1, source_target_pairs={{0,16},{8,24},{16,32},{24,40},{32,48},{40,56},{48,64},{56,72},{64,... | collective-permute-start | bytes 786440 | tf_op jit(solution)/shard_map/ppermute | solution.py:120
  14.8 19.6 %collective-permute-start.1 = (bf16[128,1024]{1,0:T(8,128)(2,1)S(1)}, bf16[128,1024]{1,0:T(8,128)(2,1)S(1)}, u32[]{:S(2)}, u32[]{:S(2)}) collective-permute-start(bf16[128,1024]{1,0:T(8,128)(2,1)S(1)} %pad_maximum_fusion.kv0_ref), channel_id=1, source_target_pairs={{0,8},{8,32},{16,24},{24,48},{32,40},{40,64},{48,56},{56,80},{64,7... | collective-permute-start | bytes 786440 | tf_op jit(solution)/shard_map/ppermute | solution.py:121
  21.5 1.0 %copy-start.3 = (bf16[1,128,2048]{2,1,0:T(8,128)(2,1)S(1)}, bf16[1,128,2048]{2,1,0:T(8,128)(2,1)}, u32[]{:S(2)}) copy-start(bf16[1,128,2048]{2,1,0:T(8,128)(2,1)} %param.8) | copy-start | bytes 1572868
  29.7 38.1 %copy-start.2 = (bf16[1,128,2048]{2,1,0:T(8,128)(2,1)S(1)}, bf16[1,128,2048]{2,1,0:T(8,128)(2,1)}, u32[]{:S(2)}) copy-start(bf16[1,128,2048]{2,1,0:T(8,128)(2,1)} %param.11) | copy-start | bytes 1572868
  29.7 5.6 %collective-permute-start.2 = (bf16[128,1024]{1,0:T(8,128)(2,1)S(1)}, bf16[128,1024]{1,0:T(8,128)(2,1)S(1)}, u32[]{:S(2)}, u32[]{:S(2)}) collective-permute-start(bf16[128,1024]{1,0:T(8,128)(2,1)S(1)} %shard_map.96.kv1_ref), channel_id=1, source_target_pairs={{0,8},{8,0},{16,24},{24,16},{32,40},{40,32},{48,56},{56,48},{64,72... | collective-permute-start | bytes 786440 | tf_op jit(solution)/shard_map/ppermute | solution.py:131
  35.3 0.7 copy-start.5
  39.2 19.8 %collective-permute-start.3 = (bf16[128,2048]{1,0:T(8,128)(2,1)S(1)}, bf16[128,2048]{1,0:T(8,128)(2,1)S(1)}, u32[]{:S(2)}, u32[]{:S(2)}) collective-permute-start(bf16[128,2048]{1,0:T(8,128)(2,1)S(1)} %get-tuple-element.4.tokens_ref), channel_id=1, source_target_pairs={{0,128},{8,24},{16,144},{24,8},{32,160},{40,56},{48,176},{56,40},{... | collective-permute-start | bytes 1572872 | tf_op jit(solution)/shard_map/ppermute | solution.py:157
  41.1 16.7 %all-to-all-start = ((f32[64,1,128]{2,1,0:T(1,128)}), f32[64,1,128]{2,1,0:T(1,128)S(1)}, u32[]{:S(2)}, u32[]{:S(2)}) async-start(f32[64,1,128]{2,1,0:T(1,128)} %bitcast.7), calls=%async_computation | async-start | bytes 65536 | tf_op jit(solution)/shard_map/all_to_all | solution.py:158
  59.0 0.7 copy-start.4
  61.5 2.2 %copy-start = (bf16[2048,1024]{1,0:T(8,128)(2,1)S(1)}, bf16[2048,1024]{1,0:T(8,128)(2,1)}, u32[]{:S(2)}) copy-start(bf16[2048,1024]{1,0:T(8,128)(2,1)} %all-gather.2.cloned.1.call-done.weight_ref) | copy-start | bytes 12582916
  63.6 4.2 %copy-start.1 = (bf16[2048,1024]{1,0:T(8,128)(2,1)S(1)}, bf16[2048,1024]{1,0:T(8,128)(2,1)}, u32[]{:S(2)}) copy-start(bf16[2048,1024]{1,0:T(8,128)(2,1)} %all-gather.2.cloned.1.call-done.weight_ref) | copy-start | bytes 12582916
  64.4 7.5 %collective-permute-start.4 = (bf16[128,1024]{1,0:T(8,128)(2,1)S(1)}, bf16[128,1024]{1,0:T(8,128)(2,1)S(1)}, u32[]{:S(2)}, u32[]{:S(2)}) collective-permute-start(bf16[128,1024]{1,0:T(8,128)(2,1)S(1)} %shard_map.101), channel_id=1, source_target_pairs={{0,128},{8,24},{16,144},{24,8},{32,160},{40,56},{48,176},{56,40},{... | collective-permute-start | bytes 786440 | tf_op jit(solution)/shard_map/ppermute | solution.py:176
Sparse Core Ops, SparseCore 0:
  10.7 50.7 all-gather.1
